TPU v7x, 512 devices: a whole 4x4x16 slice. The times are simulated.
512 devices in a mesh: region: 16 (over y, x), shard: 32 (over z, core).
Axes of the slice: x: 4, y: 4, z: 16, core: 2. Of those that a mesh axis runs over, the one named last changes fastest.
Arguments:
- tiles: bfloat16 [524288, 512], P(('region', 'shard')), may hold values from -6 to 6
- tile_block: int32 [524288], P(('region', 'shard')), may hold values from 0 to 15
- neighbors: int32 [8192, 64], P(('region', 'shard')), may hold values from 0 to 8191, as said below
- counts: int32 [8192], P(('region', 'shard')), may hold values from 1 to 64, as said below
- flows: int32 [8192, 64], P(('region', 'shard')), may hold values from 0 to 22, as said below
- w_anchor: bfloat16 [512, 1024], P('shard'), may hold values from -0.25 to 0.25
- w_dest: bfloat16 [512, 1024], P('shard'), may hold values from -0.25 to 0.25
- w_hidden: bfloat16 [1024, 1024], P('shard'), may hold values from -0.1875 to 0.1875
- w_out: bfloat16 [1024], replicated, may hold values from -0.1875 to 0.1875
Outputs:
- hidden_grad: float32 [1024, 1024], P('shard')
- out_grad: float32 [1024], replicated
- loss: float32 [], replicated
Inputs may be any that keep to these rules, and one draw needn't show every extreme that they name: `neighbors`: every destination lies in the anchor's region, at most 32 blocks from the anchor in the region's order; the first counts slots hold distinct blocks, the others hold the anchor itself. `counts`: some anchor of every region has all 64 slots valid. `flows`: zero in slots at or beyond the anchor's count; the first slot holds at least one trip.
All inputs are finite; a program needn't handle non-finite values.
Results may differ from a plain program's by a relative error of at most 0.017.
Values may be sent and summed in bfloat16 or wider, within the bound.
A program may use at most 64 MiB of HBM per device.

v0:
```python
import jax
import jax.numpy as jnp
from jax import lax
from jax.sharding import PartitionSpec as P


def shifted(array, axis, by):
    devices = lax.axis_size(axis)
    pairs = [(i, i + by) for i in range(devices) if 0 <= i + by < devices]
    return lax.ppermute(array, axis, pairs)


def shards(tiles, tile_block, neighbors, counts, flows, w_anchor, w_dest, w_hidden, w_out):
    blk = counts.shape[0]
    slots = neighbors.shape[1]
    pairs = blk * slots
    onehot = (tile_block[None, :] == jnp.arange(blk, dtype=jnp.int32)[:, None]).astype(jnp.bfloat16)
    sums = jnp.dot(onehot, tiles, preferred_element_type=jnp.float32)
    scale = lax.rsqrt(jnp.mean(sums * sums, axis=-1, keepdims=True) + 1e-05)
    features = (sums * scale).astype(jnp.bfloat16)
    w_orig_all, w_dest_all, w_hid_all = (
        lax.all_gather(w_anchor, "shard", axis=0, tiled=True),
        lax.all_gather(w_dest, "shard", axis=0, tiled=True),
        lax.all_gather(w_hidden, "shard", axis=0, tiled=True),
    )
    hidden = w_hid_all.shape[1]
    shard_pos = lax.axis_index("shard")
    region_size = blk * lax.axis_size("shard")
    local_ids = neighbors % region_size
    pieces = []
    for step in (2, 1):
        pieces.append(shifted(features, "shard", step))
    pieces.append(features)
    for step in (-1, -2):
        pieces.append(shifted(features, "shard", step))
    window = jnp.concatenate(pieces, axis=0)
    dest_slot = local_ids - (shard_pos - 2) * blk
    anchor_proj = jnp.dot(features, w_orig_all, preferred_element_type=jnp.float32)
    dest_proj = jnp.dot(window, w_dest_all, preferred_element_type=jnp.float32)
    valid = jnp.arange(slots, dtype=jnp.int32)[None, :] < counts[:, None]
    weight_out = w_out.astype(jnp.float32)
    flow_f = flows.astype(jnp.float32)
    total = lax.psum(jnp.sum(flow_f), ("region", "shard"))
    first = jnp.maximum(anchor_proj[:, None, :] + dest_proj[dest_slot], 0.0).astype(jnp.bfloat16)
    first = first.reshape(pairs, hidden)
    active = jnp.maximum(jnp.dot(first, w_hid_all, preferred_element_type=jnp.float32), 0.0)
    scores = jnp.sum(active * weight_out, axis=-1).reshape(blk, slots)
    masked = jnp.where(valid, scores, -jnp.inf)
    top = jnp.max(masked, axis=-1, keepdims=True)
    expo = jnp.where(valid, jnp.exp(scores - top), 0.0)
    mass = jnp.sum(expo, axis=-1, keepdims=True)
    probs = expo / mass
    logp = scores - top - jnp.log(mass)
    anchor_total = jnp.sum(flow_f, axis=-1, keepdims=True)
    sgrad = (jnp.where(valid, probs * anchor_total - flow_f, 0.0) / total).reshape(pairs)
    numer = -jnp.sum(jnp.where(valid, flow_f * logp, 0.0))
    sgrad, numer = (sgrad, numer)
    pre = (sgrad[:, None] * weight_out * (active > 0)).astype(jnp.bfloat16)
    grad = lax.dot_general(first, pre, (((0,), (0,)), ((), ())), preferred_element_type=jnp.float32)
    gout = jnp.sum(sgrad[:, None] * active, axis=0)
    numer_all, out_grad = lax.psum((numer, gout), ("region", "shard"))
    partial_rows = lax.psum_scatter(grad, "shard", scatter_dimension=0, tiled=True)
    hidden_grad = lax.psum(partial_rows, "region")
    return (hidden_grad, out_grad, numer_all / total)


def solution(mesh):
    return jax.shard_map(
        shards,
        mesh=mesh,
        in_specs=(
            P(("region", "shard"), None),
            P(("region", "shard")),
            P(("region", "shard"), None),
            P(("region", "shard")),
            P(("region", "shard"), None),
            P("shard", None),
            P("shard", None),
            P("shard", None),
            P(),
        ),
        out_specs=(P("shard", None), P(), P()),
        check_vma=False,
    )
```

profile of v0, /device:TPU:1, one launch (start us, length us, event | category | flops | bytes accessed | tf_op | source)
XLA Modules:
  0.0 573.3 jit_solution(5957968476530868401)
XLA Ops:
  8.0 0.7 all-gather.4.cloned.1.call-update
  9.5 1.0 multiply_reduce_fusion.2
  10.6 4.4 collective-permute-start
  15.0 4.4 collective-permute-start.1
  19.4 2.6 collective-permute-start.2
  22.0 1.3 collective-permute-start.3
  23.3 0.7 compare_select_fusion
  24.9 1.8 collective-permute-done.3
  26.7 59.8 %all-gather.6.cloned.1.call-done = bf16[512,1024]{1,0:T(8,128)(2,1)} async-done(((bf16[16,1024]{1,0:T(8,128)(2,1)}), bf16[512,1024]{1,0:T(8,128)(2,1)}) %all-gather.6.cloned.1.call-update) | async-done | bytes 1048592 | tf_op jit(solution)/shard_map/all_gather | solution.py:23
  86.5 1.5 fusion.11
  88.1 5.4 gather_fusion
  93.5 63.0 %all-gather.4.cloned.1.call-done = bf16[512,1024]{1,0:T(8,128)(2,1)} async-done(((bf16[16,1024]{1,0:T(8,128)(2,1)}), bf16[512,1024]{1,0:T(8,128)(2,1)}) %all-gather.4.cloned.1.call-update) | async-done | bytes 1048592 | tf_op jit(solution)/shard_map/all_gather | solution.py:22
  156.5 1.5 fusion.10
  158.0 2.8 maximum_convert_fusion
  160.8 66.8 %all-gather.8.cloned.1.call-done = bf16[1024,1024]{1,0:T(8,128)(2,1)} async-done(((bf16[32,1024]{1,0:T(8,128)(2,1)}), bf16[1024,1024]{1,0:T(8,128)(2,1)}) %all-gather.8.cloned.1.call-update) | async-done | bytes 2097168 | tf_op jit(solution)/shard_map/all_gather | solution.py:24
  227.6 5.9 %multiply_reduce_fusion.1 = (f32[1024]{0:T(1024)S(1)}, f32[1024,1024]{1,0:T(8,128)}) fusion(f32[1024]{0:T(1024)S(1)} %convert_element_type.24, bf16[1024,1024]{1,0:T(8,128)(2,1)S(1)} %bitcast.11, bf16[1024,1024]{1,0:T(8,128)(2,1)} %all-gather.8.cloned.1.call-done), kind=kOutput, calls=%fused_computation.3 | convolution fusion | flops 2150628352 | bytes 8396800 | tf_op jit(solution)/shard_map/dot_general | solution.py:46
  234.6 103.1 %psum.28 = f32[]{:T(128)} all-reduce(f32[]{:T(128)} %get-tuple-element.4), channel_id=1, replica_groups=mesh['region'=16,'shard'=32] {'region','shard'}, use_global_device_ids=true, to_apply=%region_6.7 | all-reduce | flops 1 | bytes 8 | tf_op jit(solution)/shard_map/psum | solution.py:43
  337.7 0.7 select_divide_fusion
  338.5 6.7 %fusion = f32[1024,1024]{1,0:T(8,128)} fusion(bf16[1024,1024]{1,0:T(8,128)(2,1)S(1)} %bitcast.12, f32[1024,1024]{1,0:T(8,128)} %get-tuple-element.11, f32[1024]{0:T(1024)S(1)} %mul.63, f32[1024]{0:T(1024)S(1)} %convert_element_type.24), kind=kOutput, calls=%fused_computation.5 | convolution fusion | flops 2151677952 | bytes 10493952 | tf_op jit(solution)/shard_map/dot_general | solution.py:59
  345.3 103.5 %reduce-scatter.2.cloned.1.call-done = f32[32,1024]{1,0:T(8,128)} async-done(((f32[1024,1024]{1,0:T(8,128)}), f32[32,1024]{1,0:T(8,128)}) %reduce-scatter.2.cloned.1.call-update) | async-done | bytes 131088 | tf_op jit(solution)/shard_map/reduce_scatter | solution.py:62
  448.9 2.7 multiply_reduce_fusion
  452.2 106.3 %all-reduce = (f32[1024]{0:T(1024)}, f32[]{:T(128)}) all-reduce(f32[1024]{0:T(1024)S(1)} %multiply_reduce_fusion, f32[]{:T(128)S(6)} %neg.3), channel_id=1, replica_groups=mesh['region'=16,'shard'=32] {'region','shard'}, use_global_device_ids=true, to_apply=%region_10.11 | all-reduce | flops 1025 | bytes 8200 | tf_op jit(solution)/shard_map/psum | solution.py:61
  559.8 4.3 all-reduce.3.cloned.1.call-done
  564.1 1.6 copy.17
  (34 shorter events, 3.7 us)
Async XLA Ops:
  7.2 2.3 copy-start
  7.2 79.4 %all-gather.6.cloned.1.call-start = ((), (), s32[]{:S(2)}) async-start(), calls=%async_computation.2 | async-start | bytes 1081344 | tf_op jit(solution)/shard_map/all_gather | solution.py:23
  7.9 148.6 %all-gather.4.cloned.1.call-start = ((), (), s32[]{:S(2)}) async-start(), calls=%async_computation.1 | async-start | bytes 1081344 | tf_op jit(solution)/shard_map/all_gather | solution.py:22
  8.7 219.0 %all-gather.8.cloned.1.call-start = ((), (), s32[]{:S(2)}) async-start(), calls=%async_computation.3 | async-start | bytes 2162688 | tf_op jit(solution)/shard_map/all_gather | solution.py:24
  9.4 439.4 %reduce-scatter.2.cloned.1.call-start = ((), (), s32[]{:S(2)}) async-start(), calls=%async_computation.4 | async-start | bytes 4325376 | tf_op jit(solution)/shard_map/reduce_scatter | solution.py:62
  10.6 14.2 %collective-permute-start = (bf16[16,512]{1,0:T(8,128)(2,1)S(1)}, bf16[16,512]{1,0:T(8,128)(2,1)S(1)}, u32[]{:S(2)}, u32[]{:S(2)}) collective-permute-start(bf16[16,512]{1,0:T(8,128)(2,1)S(1)} %multiply_convert_fusion), channel_id=1, source_target_pairs={{0,2},{1,3},{2,4},{3,5},{4,6},{5,7},{6,8},{7,9},{8,10},{9,11},{10,... | collective-permute-start | bytes 49160 | tf_op jit(solution)/shard_map/ppermute | solution.py:10
  15.0 9.8 %collective-permute-start.1 = (bf16[16,512]{1,0:T(8,128)(2,1)S(1)}, bf16[16,512]{1,0:T(8,128)(2,1)S(1)}, u32[]{:S(2)}, u32[]{:S(2)}) collective-permute-start(bf16[16,512]{1,0:T(8,128)(2,1)S(1)} %multiply_convert_fusion), channel_id=1, source_target_pairs={{0,1},{1,2},{2,3},{3,4},{4,5},{5,6},{6,7},{7,8},{8,9},{9,10},{10,1... | collective-permute-start | bytes 49160 | tf_op jit(solution)/shard_map/ppermute | solution.py:10
  19.4 5.5 collective-permute-start.2
  22.0 4.7 collective-permute-start.3
  227.6 5.9 %copy-start.2 = (s32[16]{0:T(128)S(1)}, s32[16]{0:T(128)}, u32[]{:S(2)}) copy-start(s32[16]{0:T(128)} %param.12) | copy-start | bytes 196
  227.6 6.3 %copy-start.1 = (s32[16,64]{1,0:T(8,128)S(1)}, s32[16,64]{1,0:T(8,128)}, u32[]{:S(2)}) copy-start(s32[16,64]{1,0:T(8,128)} %param.13) | copy-start | bytes 12292
  345.3 218.8 %all-reduce.3.cloned.1.call-start = ((), (), s32[]{:S(2)}) async-start(), calls=%async_computation.5 | async-start | bytes 262144 | tf_op jit(solution)/shard_map/psum | solution.py:63
Sparse Core Ops, SparseCore 0:
  10.1 76.3 all-gather.5
  88.7 67.8 all-gather.3
  158.6 68.9 all-gather.7
  345.4 103.3 reduce-scatter.1
  451.9 112.2 all-reduce.2
where the time goes:
time: 574 us; the launch traced here: 573 us
  waiting for transfers between devices  301 us (52%)
  blocking collectives  209 us (36%)
  between operations  17 us (3%)
  matrix products  16.7 us (3%)
  starting transfers between devices  12.9 us (2%)
  other arithmetic  8.82 us (2%)
  local copies, waits for them, and re-layouts  7.24 us (1%)
    psum x1, blocking collectives, shards(): numer_all, out_grad = lax.psum((numer, gout), ('region', 'shard'))  106 us
    reduce_scatter x1, waiting for transfers between devices, shards(): lax.psum_scatter(grad, 'shard', scatter_dimension=0, tiled=True)  104 us
    psum x1, blocking collectives, shards(): total = lax.psum(jnp.sum(flow_f), ('region', 'shard'))  103 us
    all_gather x1, waiting for transfers between devices, shards(): lax.all_gather(w_hidden, 'shard', axis=0, tiled=True)  66.8 us
    all_gather x1, waiting for transfers between devices, shards(): lax.all_gather(w_anchor, 'shard', axis=0, tiled=True)  63 us
    all_gather x1, waiting for transfers between devices, shards(): lax.all_gather(w_dest, 'shard', axis=0, tiled=True)  59.8 us
    ppermute x4, starting transfers between devices, shifted(): return lax.ppermute(array, axis, pairs)  12.7 us
  transfers between devices with their start and end apart: 9, of which 6 were waited for; matrix products, arithmetic and copies ran while one was open for 3% of the time, Pallas kernels for 0%

commit v1 on v0

v1 whole, which is shorter than its diff:
```python
import functools

import jax
import jax.numpy as jnp
from jax import lax
from jax.experimental import pallas as pl
from jax.experimental.pallas import tpu as pltpu
from jax.sharding import PartitionSpec as P

MESH = pl.DeviceIdType.MESH
BF16 = jnp.bfloat16
F32 = jnp.float32
HALVES = 2


def remote(src, dst, send, recv, where):
    return pltpu.make_async_remote_copy(
        src_ref=src, dst_ref=dst, send_sem=send, recv_sem=recv, device_id=where, device_id_type=MESH
    )


def step_kernel(
    dims,
    tiles, tile_block, neighbors, counts, flows, w_anchor, w_dest, w_hidden, w_out,
    grad_out, gout_out, loss_out,
    pair_w, hid_w, window, proj, onehot, first_t, active, pre, grad, sib_grad, chip_grad, plane_in, plane_sum,
    z_in, own_rows, extra, extra_z, extra_zsum, extra_plane, extra_psum, extra_sib,
    ring_r_send, ring_r_recv, ring_l_send, ring_l_recv, pair_send, pair_recv, halo_send, halo_recv,
    hz_send, hz_recv, hp_send, hp_recv, hs_send, hs_recv, gs_send, gs_recv, gp_send, gp_recv, gz_send, gz_recv,
    ga_send, ga_recv, ez_send, ez_recv, ep_send, ep_recv, es_send, es_recv, local_sem,
):
    planes, depth, blk, slots, hid = dims
    pos = lax.axis_index("shard")
    mine = lax.axis_index("region")
    z, core = pos // 2, pos % 2
    shards = 2 * depth
    cols = hid // (planes // HALVES)
    feat = tiles.shape[1]
    half, block = mine // (planes // HALVES), mine % (planes // HALVES)

    def plane_peer(i):
        return lax.rem(mine + i, planes)

    def z_peer(i):
        return lax.rem(z + i, depth)

    def at_z(where):
        return {"shard": where * 2 + core}

    sibling = {"shard": z * 2 + (1 - core)}
    cross = {"shard": lax.rem(pos + shards + 2 * core - 1, shards)}

    barrier = pltpu.get_barrier_semaphore()
    pl.semaphore_signal(barrier, inc=1, device_id=sibling, device_id_type=MESH)
    pl.semaphore_signal(barrier, inc=1, device_id=cross, device_id_type=MESH)

    def greet_z(i, c):
        pl.semaphore_signal(barrier, inc=1, device_id=at_z(z_peer(i)), device_id_type=MESH)
        return c

    def greet_plane(i, c):
        pl.semaphore_signal(barrier, inc=1, device_id={"region": plane_peer(i)}, device_id_type=MESH)
        return c

    lax.fori_loop(1, depth, greet_z, 0)
    lax.fori_loop(1, planes, greet_plane, 0)

    pair_w[z, core, 0] = w_anchor[...]
    pair_w[z, core, 1] = w_dest[...]

    def hid_tile(ref, row, p):
        r = pl.multiple_of(row + (p // (planes // HALVES)) * 16, 16)
        c = pl.multiple_of((p % (planes // HALVES)) * cols, cols)
        return ref.at[:, pl.ds(r, 16), pl.ds(c, cols)]

    def hid_tile_z(ref, where, row, p):
        r = pl.multiple_of(row + (p // (planes // HALVES)) * 16, 16)
        c = pl.multiple_of((p % (planes // HALVES)) * cols, cols)
        return ref.at[where, pl.ds(r, 16), pl.ds(c, cols)]

    own_r = pl.multiple_of(half * 16, 16)
    own_c = pl.multiple_of(block * cols, cols)
    own_tile = w_hidden.at[pl.ds(own_r, 16), pl.ds(own_c, cols)]
    tile_copy = pltpu.make_async_copy(own_tile, hid_tile_z(hid_w, z, core * 32, mine), local_sem.at[0])
    tile_copy.start()

    member = tile_block[...] == lax.broadcasted_iota(jnp.int32, (blk, tile_block.shape[1]), 0)
    sums = jnp.dot(member.astype(BF16), tiles[...], preferred_element_type=F32)
    scale = lax.rsqrt(jnp.mean(sums * sums, axis=-1, keepdims=True) + 1e-05)
    window[2] = (sums * scale).astype(BF16)
    tile_copy.wait()

    pl.semaphore_wait(barrier, planes - 1 + depth - 1 + 2)

    hops_r, hops_l = depth // 2, (depth - 1) // 2

    def ring(where, to, send, recv):
        return remote(pair_w.at[where, core], pair_w.at[where, core], send, recv, at_z(to))

    def ring_right(t):
        return ring(lax.rem(z - t + 2 * depth, depth), z_peer(1), ring_r_send.at[t], ring_r_recv.at[t])

    def ring_left(t):
        return ring(z_peer(t), lax.rem(z + depth - 1, depth), ring_l_send.at[t], ring_l_recv.at[t])

    def hand_pair(where):
        return remote(
            pair_w.at[where, core], pair_w.at[where, core], pair_send.at[where], pair_recv.at[where], sibling
        )

    def take_pair(where):
        return remote(
            pair_w.at[where, 1 - core], pair_w.at[where, 1 - core], pair_send.at[where], pair_recv.at[where], sibling
        )

    ring_right(0).start()
    if hops_l:
        ring_left(0).start()

    def hid_z(i):
        return remote(
            own_tile, hid_tile_z(hid_w, z, core * 32, mine), hz_send.at[i], hz_recv.at[i], at_z(z_peer(i))
        )

    def hid_z_from(i):
        where = lax.rem(z - i + 2 * depth, depth)
        return remote(own_tile, hid_tile_z(hid_w, where, core * 32, mine), hz_send.at[i], hz_recv.at[i], at_z(where))

    lax.fori_loop(1, depth, lambda i, c: (hid_z(i).start(), c)[1], 0)
    hand_pair(z).start()

    def halo(by):
        return remote(
            window.at[2], window.at[2 - by], halo_send.at[by + 2], halo_recv.at[by + 2],
            {"shard": lax.rem(pos + by + shards, shards)},
        )

    for by in (-2, -1, 1, 2):
        halo(by).start()

    shift = mine * (blk * shards) + (pos - 2) * blk
    place = (neighbors[...] - shift).astype(F32).T
    flow = flows[...].astype(F32).T
    lane16 = lax.broadcasted_iota(jnp.int32, (slots, blk), 1)
    count = jnp.zeros((1, blk), jnp.int32)
    for b in range(blk):
        count = jnp.where(lax.broadcasted_iota(jnp.int32, (1, blk), 1) == b, counts[b], count)
    valid = lax.broadcasted_iota(jnp.int32, (slots, blk), 0) < count
    lane = lax.broadcasted_iota(jnp.int32, (slots, 128), 1).astype(F32)
    for b in range(blk):
        here = (lane == place[:, b:b + 1]) | (lane == 5 * blk + b)
        onehot[b * slots:(b + 1) * slots, :] = jnp.where(here, 1.0, 0.0).astype(BF16)
    anchor_total = jnp.sum(flow, axis=0, keepdims=True)
    proj[...] = jnp.zeros_like(proj)

    def hid_p(i):
        tile = hid_tile(hid_w, core * 32, mine)
        return remote(tile, tile, hp_send.at[i], hp_recv.at[i], {"region": plane_peer(i)})

    def hid_p_from(i):
        p = lax.rem(mine - i + 2 * planes, planes)
        tile = hid_tile(hid_w, core * 32, p)
        return remote(tile, tile, hp_send.at[i], hp_recv.at[i], {"region": p})

    def hand_hid(i):
        tile = hid_tile(hid_w, core * 32, lax.rem(mine - i + 2 * planes, planes))
        return remote(tile, tile, hs_send.at[i], hs_recv.at[i], sibling)

    def take_hid(i):
        tile = hid_tile(hid_w, (1 - core) * 32, lax.rem(mine - i + 2 * planes, planes))
        return remote(tile, tile, hs_send.at[i], hs_recv.at[i], sibling)

    def ring_step(t):
        ring_right(t - 1).wait_send()
        take = ring(lax.rem(z - t + 2 * depth, depth), z_peer(1), ring_r_send.at[t - 1], ring_r_recv.at[t - 1])
        take.wait_recv()
        if t < hops_r:
            ring_right(t).start()
        hand_pair(lax.rem(z - t + 2 * depth, depth)).start()
        if t <= hops_l:
            ring_left(t - 1).wait_send()
            take = ring(z_peer(t), z_peer(1), ring_l_send.at[t - 1], ring_l_recv.at[t - 1])
            take.wait_recv()
            if t < hops_l:
                ring_left(t).start()
            hand_pair(z_peer(t)).start()

    def hid_step(i):
        hid_p_from(i).wait_recv()
        hand_hid(i).start()

    ring_step(1)
    lax.fori_loop(1, depth, lambda i, c: (hid_z_from(i).wait_recv(), c)[1], 0)
    lax.fori_loop(1, planes, lambda i, c: (hid_p(i).start(), c)[1], 0)
    hand_hid(0).start()
    done = 1
    for t in range(2, hops_r + 1):
        ring_step(t)
        for i in range(done, min(done + 2, planes)):
            hid_step(i)
        done = min(done + 2, planes)

    lax.fori_loop(0, depth, lambda i, c: (take_pair(i).wait_recv(), c)[1], 0)
    for by in (-2, -1, 1, 2):
        halo(by).wait_recv()

    rows = 5 * blk
    dest = jnp.dot(
        window[...].reshape(rows, feat), pair_w[:, :, 1].reshape(feat, hid), preferred_element_type=F32
    )
    dest_top = dest.astype(BF16)
    proj[0:rows] = dest_top
    proj[128:128 + rows] = (dest - dest_top.astype(F32)).astype(BF16)
    anchor = jnp.dot(window[2], pair_w[:, :, 0].reshape(feat, hid), preferred_element_type=F32)
    anchor_top = anchor.astype(BF16)
    proj[rows:rows + blk] = anchor_top
    proj[128 + rows:128 + rows + blk] = (anchor - anchor_top.astype(F32)).astype(BF16)

    for i in range(done, planes):
        hid_step(i)
    lax.fori_loop(0, planes, lambda i, c: (take_hid(i).wait_recv(), c)[1], 0)

    group = 4
    size = group * slots
    weight = w_out[...].astype(F32)

    def score(i, scores):
        at = pl.multiple_of(i * size, size)
        pick = onehot[pl.ds(at, size), :]
        both = jnp.concatenate([pick, pick], axis=1)
        first = jnp.maximum(jnp.dot(both, proj[...], preferred_element_type=F32), 0.0).astype(BF16)
        first_t[:, pl.ds(at, size)] = first.T
        act = jnp.maximum(
            jnp.dot(first, hid_w[...].reshape(hid, hid), preferred_element_type=F32), 0.0
        )
        active[pl.ds(at, size), :] = act
        col = jnp.sum(act * weight, axis=1, keepdims=True)
        for a in range(group):
            scores = jnp.where(lane16 == i * group + a, col[a * slots:(a + 1) * slots], scores)
        return scores

    scores = lax.fori_loop(0, blk // group, score, jnp.zeros((slots, blk), F32))

    top = jnp.max(jnp.where(valid, scores, -jnp.inf), axis=0, keepdims=True)
    expo = jnp.where(valid, jnp.exp(scores - top), 0.0)
    mass = jnp.sum(expo, axis=0, keepdims=True)
    probs = expo / mass
    logp = scores - top - jnp.log(mass)
    sgrad = jnp.where(valid, probs * anchor_total - flow, 0.0)
    numer = -jnp.sum(jnp.where(valid, flow * logp, 0.0))
    total = jnp.sum(anchor_total)

    def back(i, gout):
        at = pl.multiple_of(i * size, size)
        col = jnp.concatenate(
            [
                jnp.sum(jnp.where(lane16 == i * group + a, sgrad, 0.0), axis=1, keepdims=True)
                for a in range(group)
            ],
            axis=0,
        )
        act = active[pl.ds(at, size), :]
        pre[pl.ds(at, size), :] = jnp.where(act > 0, col * weight, 0.0).astype(BF16)
        return gout + jnp.sum((col * act).reshape(size // 8, 8, hid), axis=0)

    gout = lax.fori_loop(0, blk // group, back, jnp.zeros((8, hid), F32))
    gout = jnp.sum(gout, axis=0, keepdims=True)

    width = hid // 8
    for r in range(8):
        extra[r:r + 1, :] = gout[:, r * width:(r + 1) * width]
    row = lax.broadcasted_iota(jnp.int32, (8, width), 0)
    extra[8:16, :] = jnp.where(row == 0, numer, jnp.where(row == 1, total, 0.0))

    def extra_to_z(i):
        return remote(extra, extra_z.at[z], ez_send.at[i], ez_recv.at[i], at_z(z_peer(i)))

    def extra_from_z(i):
        where = lax.rem(z - i + 2 * depth, depth)
        return remote(extra, extra_z.at[where], ez_send.at[i], ez_recv.at[i], at_z(where))

    def extra_to_plane(i):
        return remote(extra_zsum, extra_plane.at[mine], ep_send.at[i], ep_recv.at[i], {"region": plane_peer(i)})

    def extra_from_plane(i):
        p = lax.rem(mine - i + 2 * planes, planes)
        return remote(extra_zsum, extra_plane.at[p], ep_send.at[i], ep_recv.at[i], {"region": p})

    lax.fori_loop(1, depth, lambda i, c: (extra_to_z(i).start(), c)[1], 0)
    extra_z[z] = extra[...]

    wide = 2 * cols
    turns = hid // wide

    def turn(n):
        return pl.multiple_of(lax.rem(block // 2 + 1 + n, turns) * wide, wide)

    def to_sibling(n):
        rows_of = pl.ds(pl.multiple_of((1 - core) * 32, 32), 32)
        return remote(
            grad.at[:, rows_of, pl.ds(turn(n), wide)], sib_grad.at[:, :, pl.ds(turn(n), wide)],
            gs_send.at[n], gs_recv.at[n], sibling,
        )

    def grads(n, c):
        part = jnp.dot(first_t[...], pre[:, pl.ds(turn(n), wide)], preferred_element_type=F32)
        grad[:, :, pl.ds(turn(n), wide)] = part.reshape(depth, hid // depth, wide).astype(BF16)
        to_sibling(n).start()
        return c

    lax.fori_loop(0, turns, grads, 0)

    lax.fori_loop(1, depth, lambda i, c: (extra_from_z(i).wait_recv(), c)[1], 0)
    extra_zsum[...] = jnp.sum(extra_z[...], axis=0)
    lax.fori_loop(1, planes, lambda i, c: (extra_to_plane(i).start(), c)[1], 0)
    extra_plane[mine] = extra_zsum[...]

    def to_plane(p):
        return remote(
            hid_tile(chip_grad, 0, p), plane_in.at[mine], gp_send.at[p], gp_recv.at[mine], {"region": p}
        )

    def from_plane(p):
        return remote(hid_tile(chip_grad, 0, mine), plane_in.at[p], gp_send.at[p], gp_recv.at[p], {"region": p})

    def join(n, c):
        to_sibling(n).wait_recv()
        at = turn(n)
        mine_part = grad[:, pl.ds(pl.multiple_of(core * 32, 32), 32), pl.ds(at, wide)].astype(F32)
        chip_grad[:, :, pl.ds(at, wide)] = (mine_part + sib_grad[:, :, pl.ds(at, wide)].astype(F32)).astype(BF16)
        for h in range(HALVES):
            for b in range(2):
                p = h * (planes // HALVES) + at // cols + b

                @pl.when(p != mine)
                def _():
                    to_plane(p).start()
        return c

    lax.fori_loop(0, turns, join, 0)
    own_part = pltpu.make_async_copy(hid_tile(chip_grad, 0, mine), plane_in.at[mine], local_sem.at[1])
    own_part.start()
    own_part.wait()

    lax.fori_loop(1, planes, lambda i, c: (extra_from_plane(i).wait_recv(), c)[1], 0)
    extra_psum[...] = jnp.sum(extra_plane[...], axis=0)
    extra_swap = remote(extra_psum, extra_sib, es_send, es_recv, sibling)
    extra_swap.start()

    lax.fori_loop(1, planes, lambda i, c: (from_plane(plane_peer(i)).wait_recv(), c)[1], 0)

    def to_z(i):
        return remote(plane_sum.at[z_peer(i)], z_in.at[z], gz_send.at[i], gz_recv.at[i], at_z(z_peer(i)))

    def from_z(i):
        where = lax.rem(z - i + 2 * depth, depth)
        return remote(plane_sum.at[where], z_in.at[where], gz_send.at[i], gz_recv.at[i], at_z(where))

    def plane_total(where):
        acc = plane_in[0, where].astype(F32)
        for p in range(1, planes):
            acc = acc + plane_in[p, where].astype(F32)
        return acc.astype(BF16)

    def spread(i, c):
        plane_sum[z_peer(i)] = plane_total(z_peer(i))
        to_z(i).start()
        return c

    lax.fori_loop(1, depth, spread, 0)
    z_in[z] = plane_total(z)

    extra_swap.wait_recv()
    sums_all = extra_psum[...] + extra_sib[...]
    inverse = 1.0 / sums_all[9:10, :]
    gout_out[...] = sums_all[0:8, :] * inverse
    loss_out[...] = sums_all[8:9, 0:1] * inverse[:, 0:1]

    lax.fori_loop(1, depth, lambda i, c: (from_z(i).wait_recv(), c)[1], 0)
    acc = z_in[0].astype(F32)
    for i in range(1, depth):
        acc = acc + z_in[i].astype(F32)
    own_rows[...] = acc * inverse[0:1, 0:1]

    def out_tile(p):
        r = pl.multiple_of((p // (planes // HALVES)) * 16, 16)
        c = pl.multiple_of((p % (planes // HALVES)) * cols, cols)
        return grad_out.at[pl.ds(r, 16), pl.ds(c, cols)]

    def share(i):
        return remote(own_rows, out_tile(mine), ga_send.at[i], ga_recv.at[i], {"region": plane_peer(i)})

    def shared(i):
        p = lax.rem(mine - i + 2 * planes, planes)
        return remote(own_rows, out_tile(p), ga_send.at[i], ga_recv.at[i], {"region": p})

    lax.fori_loop(1, planes, lambda i, c: (share(i).start(), c)[1], 0)
    own_out = pltpu.make_async_copy(own_rows, out_tile(mine), local_sem.at[2])
    own_out.start()

    lax.fori_loop(0, depth, lambda i, c: (hand_pair(i).wait_send(), c)[1], 0)
    for by in (-2, -1, 1, 2):
        halo(by).wait_send()
    lax.fori_loop(1, depth, lambda i, c: (hid_z(i).wait_send(), c)[1], 0)
    lax.fori_loop(1, planes, lambda i, c: (hid_p(i).wait_send(), c)[1], 0)
    lax.fori_loop(0, planes, lambda i, c: (hand_hid(i).wait_send(), c)[1], 0)
    lax.fori_loop(1, depth, lambda i, c: (extra_to_z(i).wait_send(), c)[1], 0)
    lax.fori_loop(1, planes, lambda i, c: (extra_to_plane(i).wait_send(), c)[1], 0)
    extra_swap.wait_send()
    lax.fori_loop(0, turns, lambda n, c: (to_sibling(n).wait_send(), c)[1], 0)
    lax.fori_loop(1, planes, lambda i, c: (to_plane(plane_peer(i)).wait_send(), c)[1], 0)
    lax.fori_loop(1, depth, lambda i, c: (to_z(i).wait_send(), c)[1], 0)
    own_out.wait()
    lax.fori_loop(1, planes, lambda i, c: (shared(i).wait_recv(), c)[1], 0)
    lax.fori_loop(1, planes, lambda i, c: (share(i).wait_send(), c)[1], 0)


def shards(tiles, tile_block, neighbors, counts, flows, w_anchor, w_dest, w_hidden, w_out):
    planes, shard_count = lax.axis_size("region"), lax.axis_size("shard")
    depth = shard_count // 2
    blk, slots = neighbors.shape
    feat, hid = tiles.shape[1], w_hidden.shape[1]
    pairs = blk * slots
    cols = hid // (planes // HALVES)
    turns = hid // (2 * cols)
    vmem = pl.BlockSpec(memory_space=pltpu.VMEM)
    dma = lambda n: pltpu.SemaphoreType.DMA((n,))
    scratch = [
        pltpu.VMEM((depth, 2, 2, w_anchor.shape[0], hid), BF16),
        pltpu.VMEM((depth, 64, hid), BF16),
        pltpu.VMEM((5, blk, feat), BF16),
        pltpu.VMEM((256, hid), BF16),
        pltpu.VMEM((pairs, 128), BF16),
        pltpu.VMEM((hid, pairs), BF16),
        pltpu.VMEM((pairs, hid), F32),
        pltpu.VMEM((pairs, hid), BF16),
        pltpu.VMEM((depth, 64, hid), BF16),
        pltpu.VMEM((depth, 32, hid), BF16),
        pltpu.VMEM((depth, 32, hid), BF16),
        pltpu.VMEM((planes, depth, 16, cols), BF16),
        pltpu.VMEM((depth, 16, cols), BF16),
        pltpu.VMEM((depth, 16, cols), BF16),
        pltpu.VMEM((16, cols), F32),
        pltpu.VMEM((16, hid // 8), F32),
        pltpu.VMEM((depth, 16, hid // 8), F32),
        pltpu.VMEM((16, hid // 8), F32),
        pltpu.VMEM((planes, 16, hid // 8), F32),
        pltpu.VMEM((16, hid // 8), F32),
        pltpu.VMEM((16, hid // 8), F32),
        dma(depth), dma(depth), dma(depth), dma(depth), dma(depth), dma(depth), dma(5), dma(5),
        dma(depth), dma(depth), dma(planes), dma(planes), dma(planes), dma(planes),
        dma(turns), dma(turns), dma(planes), dma(planes), dma(depth), dma(depth),
        dma(planes), dma(planes), dma(depth), dma(depth), dma(planes), dma(planes),
        pltpu.SemaphoreType.DMA, pltpu.SemaphoreType.DMA, dma(3),
    ]
    grad, gout, loss = pl.pallas_call(
        functools.partial(step_kernel, (planes, depth, blk, slots, hid)),
        out_shape=(
            jax.ShapeDtypeStruct((w_hidden.shape[0], hid), F32),
            jax.ShapeDtypeStruct((8, hid // 8), F32),
            jax.ShapeDtypeStruct((1, 1), F32),
        ),
        in_specs=[vmem, vmem, vmem, pl.BlockSpec(memory_space=pltpu.SMEM), vmem, vmem, vmem, vmem, vmem],
        out_specs=(vmem, vmem, vmem),
        scratch_shapes=scratch,
        compiler_params=pltpu.CompilerParams(
            collective_id=0, has_side_effects=True, vmem_limit_bytes=50 * 2 ** 20
        ),
        cost_estimate=pl.CostEstimate(
            flops=4 * pairs * hid * hid, bytes_accessed=2 * tiles.size, transcendentals=pairs
        ),
    )(
        tiles, tile_block.reshape(1, -1), neighbors, counts, flows, w_anchor, w_dest, w_hidden, w_out.reshape(1, -1)
    )
    return grad, gout.reshape(hid), loss.reshape(())


def solution(mesh):
    return jax.shard_map(
        shards,
        mesh=mesh,
        in_specs=(
            P(("region", "shard"), None),
            P(("region", "shard")),
            P(("region", "shard"), None),
            P(("region", "shard")),
            P(("region", "shard"), None),
            P("shard", None),
            P("shard", None),
            P("shard", None),
            P(),
        ),
        out_specs=(P("shard", None), P(), P()),
        check_vma=False,
    )
```

time: 574 us -> 110 us (0.19)
  waiting for transfers between devices: 301 us -> 0 us
  blocking collectives: 209 us -> 0 us
  Pallas kernels: 0 us -> 98.7 us
  matrix products: 16.7 us -> 0 us
  between operations: 17 us -> 2.48 us
  starting transfers between devices: 12.9 us -> 0 us
  other arithmetic: 8.82 us -> 0 us
    psum x2 -> x0, blocking collectives: 209 us -> none  [the longest x1 106 us: shards(): numer_all, out_grad = lax.psum((numer, gout), ('region', 'shard'))]
    all_gather x3 -> x0, waiting for transfers between devices: 190 us -> none  [the longest x1 66.8 us: shards(): lax.all_gather(w_hidden, 'shard', axis=0, tiled=True)]
    reduce_scatter x1 -> x0, waiting for transfers between devices: 104 us -> none  [shards(): lax.psum_scatter(grad, 'shard', scatter_dimension=0, tiled=True)]
    pallas_call x0 -> x1, Pallas kernels: none -> 98.7 us  [shards(): pl.pallas_call(functools.partial(step_kernel, (planes, depth, blk, slots,...]
    dot_general x5 -> x0, matrix products: 16.7 us -> none  [the longest x1 6.74 us: shards(): lax.dot_general(first, pre, (((0,), (0,)), ((), ())), preferred_element_t...]
    ppermute x4 -> x0, starting transfers between devices: 12.7 us -> none  [shifted(): return lax.ppermute(array, axis, pairs)]
  transfers between devices with their start and end apart: 9 -> 0, of which waited for: 6 -> 0; matrix products, arithmetic and copies ran while one was open for 3% -> 0% of each run, Pallas kernels for 0% -> 0%
where the time goes in v1:
time: 110 us; the launch traced here: 108 us
  Pallas kernels  98.7 us (90%)
  local copies, waits for them, and re-layouts  6.92 us (6%)
  between operations  2.48 us (2%)
    pallas_call x1, Pallas kernels, shards(): pl.pallas_call(functools.partial(step_kernel, (planes, depth, blk, slots,...  98.7 us
    unnamed x18, local copies, waits for them, and re-layouts  6.23 us

profile of v1, /device:TPU:1, one launch (start us, length us, event | category | flops | bytes accessed | tf_op | source)
XLA Modules:
  0.0 108.2 jit_solution(8465399131231575903)
XLA Ops:
  0.6 0.0 copy-start.6
  0.6 0.0 copy-start.7
  0.7 0.7 reshape.19.w_out
  1.3 0.0 copy-done.6
  1.4 0.0 copy-done.7
  1.4 0.0 copy-start
  1.4 1.2 %copy-done = bf16[1024,512]{1,0:T(8,128)(2,1)S(1)} copy-done((bf16[1024,512]{1,0:T(8,128)(2,1)S(1)}, bf16[1024,512]{1,0:T(8,128)(2,1)}, u32[]{:S(2)}) %copy-start) | copy-done | bytes 1048600
  2.6 0.0 copy-start.1
  2.6 0.8 copy-done.1
  3.4 0.0 copy-start.2
  3.4 0.8 copy-done.2
  4.2 0.0 copy-start.3
  4.2 0.8 copy-done.3
  4.9 0.0 copy-start.4
  4.9 0.7 copy-done.4
  5.6 0.0 copy-start.5
  5.6 0.7 copy-done.5
  6.3 98.7 %shard_map.112 = (f32[32,1024]{1,0:T(8,128)S(1)}, f32[8,128]{1,0:T(8,128)S(1)}, f32[1,1]{1,0:T(1,128)}) custom-call(bf16[1024,512]{1,0:T(8,128)(2,1)S(1)} %copy-done, s32[1,1024]{1,0:T(1,128)S(1)} %bitcast.4, s32[16,64]{1,0:T(8,128)S(1)} %copy-done.4, s32[16]{0:T(128)S(1)} %copy-done.7, s32[16,64]{1,0:T(8,128)S(1)} %copy-done.5, ...), custom_call_target="tpu_custom_call" | custom-call | flops 4294967296 | bytes 1048576 | tf_op jit(solution)/shard_map/pallas_call | solution.py:456
  105.1 0.7 copy.15
  105.7 0.6 copy.16
Async XLA Ops:
  0.6 0.7 copy-start.6
  0.6 0.7 copy-start.7
  1.4 1.2 %copy-start = (bf16[1024,512]{1,0:T(8,128)(2,1)S(1)}, bf16[1024,512]{1,0:T(8,128)(2,1)}, u32[]{:S(2)}) copy-start(bf16[1024,512]{1,0:T(8,128)(2,1)} %tiles.1) | copy-start | bytes 3145732
  2.6 0.8 copy-start.1
  3.4 0.8 copy-start.2
  4.2 0.8 copy-start.3
  4.9 0.7 copy-start.4
  5.6 0.7 copy-start.5

commit v2 on v0

v2 whole, which is shorter than its diff:
```python
import functools

import jax
import jax.numpy as jnp
from jax import lax
from jax.experimental import pallas as pl
from jax.experimental.pallas import tpu as pltpu
from jax.sharding import PartitionSpec as P

MESH = pl.DeviceIdType.MESH
BF16 = jnp.bfloat16
F32 = jnp.float32


def remote(src, dst, send, recv, where):
    return pltpu.make_async_remote_copy(
        src_ref=src, dst_ref=dst, send_sem=send, recv_sem=recv, device_id=where, device_id_type=MESH
    )


def step_kernel(
    dims,
    tiles_hbm, tile_block_hbm, neighbors_hbm, counts_hbm, flows_hbm, anchor_hbm, dest_hbm, hidden_hbm, out_hbm,
    grad_out, gout_out, loss_out,
    tiles, tile_block, neighbors, counts, flows, w_out,
    own_w, weights, window, proj, onehot, first_t, active, pre, grad, sib_grad, chip_grad, u_in, u_sum, v_in,
    plane_sum, z_in, own_rows, extra, extra_z, extra_zsum, extra_plane, extra_psum, extra_sib,
    halo_send, halo_recv, az_send, az_recv, p1_send, p1_recv, p2_send, p2_recv, sb_send, sb_recv,
    gs_send, gs_recv, gu_send, gu_recv, gv_send, gv_recv, gz_send, gz_recv,
    ga_send, ga_recv, ez_send, ez_recv, ep_send, ep_recv, es_send, es_recv, load_sem, local_sem,
):
    side, depth, blk, slots, hid = dims
    planes = side * side
    pos = lax.axis_index("shard")
    mine = lax.axis_index("region")
    z, core = pos // 2, pos % 2
    shards = 2 * depth
    feat = tiles.shape[1]
    y, x = mine // side, mine % side
    u = y + core * (x - y)
    v = x + core * (y - x)
    per_half = side // 2
    group_cols = hid // per_half
    tile_cols = group_cols // side

    def wrap(i, n):
        return lax.rem(i + 2 * n, n)

    def at_z(where):
        return {"shard": where * 2 + core}

    def at_uv(uu, vv):
        return {"region": (uu * side + vv) * (1 - core) + (vv * side + uu) * core}

    sibling = {"shard": z * 2 + (1 - core)}
    cross = {"shard": wrap(pos + 2 * core - 1, shards)}

    def each(first, last, act):
        def body(i, c):
            act(i)
            return c

        lax.fori_loop(first, last, body, 0)

    loads = [
        pltpu.make_async_copy(anchor_hbm, own_w.at[0, 0], load_sem.at[0]),
        pltpu.make_async_copy(dest_hbm, own_w.at[1, 0], load_sem.at[1]),
        pltpu.make_async_copy(hidden_hbm.at[0:16], own_w.at[0, 1], load_sem.at[2]),
        pltpu.make_async_copy(hidden_hbm.at[16:32], own_w.at[1, 1], load_sem.at[3]),
        pltpu.make_async_copy(tiles_hbm, tiles, load_sem.at[4]),
        pltpu.make_async_copy(tile_block_hbm, tile_block, load_sem.at[5]),
        pltpu.make_async_copy(neighbors_hbm, neighbors, load_sem.at[6]),
        pltpu.make_async_copy(counts_hbm, counts, load_sem.at[7]),
        pltpu.make_async_copy(flows_hbm, flows, load_sem.at[8]),
        pltpu.make_async_copy(out_hbm, w_out, load_sem.at[9]),
    ]
    for copy in loads:
        copy.start()
    barrier = pltpu.get_barrier_semaphore()

    def greet(where):
        pl.semaphore_signal(barrier, inc=1, device_id=where, device_id_type=MESH)

    greet(sibling)
    greet(cross)
    each(1, depth, lambda i: greet(at_z(wrap(z + i, depth))))
    each(1, planes, lambda i: greet({"region": wrap(mine + i, planes)}))

    def span(ref, uu, first, count):
        at = (uu % per_half) * group_cols + first * tile_cols
        return pl.ds(pl.multiple_of(at, tile_cols), count * tile_cols)

    def weight_tile(where, zs):
        return weights.at[pl.ds(where, zs), core, u // per_half, :, :, span(weights, u, v, 1)]

    def weight_group(where, zs, uu, cc):
        return weights.at[pl.ds(where, zs), cc, uu // per_half, :, :, span(weights, uu, 0, side)]

    own_tile = own_w.at[u // per_half, :, :, span(own_w, u, v, 1)]

    def weight_slot(where):
        return weights.at[where, core, u // per_half, :, :, span(weights, u, v, 1)]

    def to_z_weights(i):
        to = wrap(z + i, depth)
        return remote(own_tile, weight_slot(z), az_send.at[to], az_recv.at[z], at_z(to))

    def from_z_weights(where):
        return remote(own_tile, weight_slot(where), az_send.at[where], az_recv.at[where], at_z(where))

    for copy in loads[0:4]:
        copy.wait()
    keep_tile = pltpu.make_async_copy(own_tile, weight_slot(z), local_sem.at[0])
    keep_tile.start()
    pl.semaphore_wait(barrier, planes - 1 + depth - 1 + 2)

    def both_ways(i):
        to_z_weights(i).start()
        to_z_weights(depth - i).start()

    each(1, depth // 2, both_ways)
    to_z_weights(depth // 2).start()

    for copy in loads[4:]:
        copy.wait()
    member = tile_block[...] == lax.broadcasted_iota(jnp.int32, (blk, tile_block.shape[1]), 0)
    sums = jnp.dot(member.astype(BF16), tiles[...], preferred_element_type=F32)
    scale = lax.rsqrt(jnp.mean(sums * sums, axis=-1, keepdims=True) + 1e-05)
    window[2] = (sums * scale).astype(BF16)

    def halo(by):
        return remote(
            window.at[2], window.at[2 - by], halo_send.at[by + 2], halo_recv.at[by + 2],
            {"shard": wrap(pos + by, shards)},
        )

    for by in (-2, -1, 1, 2):
        halo(by).start()

    shift = mine * (blk * shards) + (pos - 2) * blk
    place = (neighbors[...] - shift).astype(F32).T
    flow = flows[...].astype(F32).T
    lane16 = lax.broadcasted_iota(jnp.int32, (slots, blk), 1)
    count = jnp.zeros((1, blk), jnp.int32)
    for b in range(blk):
        count = jnp.where(lax.broadcasted_iota(jnp.int32, (1, blk), 1) == b, counts[b], count)
    valid = lax.broadcasted_iota(jnp.int32, (slots, blk), 0) < count
    lane = lax.broadcasted_iota(jnp.int32, (slots, 128), 1).astype(F32)
    for b in range(blk):
        here = (lane == place[:, b:b + 1]) | (lane == 5 * blk + b)
        onehot[b * slots:(b + 1) * slots, :] = jnp.where(here, 1.0, 0.0).astype(BF16)
    anchor_total = jnp.sum(flow, axis=0, keepdims=True)
    proj[...] = jnp.zeros_like(proj)
    keep_tile.wait()

    zs = depth // 4
    first_block = z // zs

    def block_at(n):
        return wrap(first_block + (0, 1, -1, 2)[n], 4)

    def along_v(b, i):
        tile = weight_tile(b * zs, zs)
        return remote(
            tile, tile, p1_send.at[b * side + i], p1_recv.at[b * side + i], at_uv(u, wrap(v + i, side))
        )

    def from_v(b, i):
        vv = wrap(v - i, side)
        tile = weights.at[pl.ds(b * zs, zs), core, u // per_half, :, :, span(weights, u, vv, 1)]
        return remote(tile, tile, p1_send.at[b * side + i], p1_recv.at[b * side + i], at_uv(u, vv))

    def along_u(b, i):
        part = weight_group(b * zs, zs, u, core)
        return remote(
            part, part, p2_send.at[b * side + i], p2_recv.at[b * side + i], at_uv(wrap(u + i, side), v)
        )

    def from_u(b, i):
        uu = wrap(u - i, side)
        part = weight_group(b * zs, zs, uu, core)
        return remote(part, part, p2_send.at[b * side + i], p2_recv.at[b * side + i], at_uv(uu, v))

    def hand(b, i):
        part = weight_group(b * zs, zs, wrap(u - i, side), core)
        return remote(part, part, sb_send.at[b * side + i], sb_recv.at[b * side + i], sibling)

    def take(b, i):
        part = weight_group(b * zs, zs, wrap(v - i, side), 1 - core)
        return remote(part, part, sb_send.at[b * side + i], sb_recv.at[b * side + i], sibling)

    for n in range(6):
        if 1 <= n <= 4:
            b = block_at(n - 1)
            for i in range(1, side):
                from_v(b, i).wait_recv()
            for i in range(1, side):
                along_u(b, i).start()
            hand(b, 0).start()
        if n < 4:
            b = block_at(n)
            for k in range(zs):

                @pl.when(b * zs + k != z)
                def _():
                    from_z_weights(b * zs + k).wait_recv()

            for i in range(1, side):
                along_v(b, i).start()
        if n >= 2:
            b = block_at(n - 2)
            for i in range(1, side):
                from_u(b, i).wait_recv()
                hand(b, i).start()

    for by in (-2, -1, 1, 2):
        halo(by).wait_recv()
    each(0, 4 * side, lambda i: take(i // side, i % side).wait_recv())

    rows = 5 * blk
    dest = jnp.dot(
        window[...].reshape(rows, feat), weights[:, :, 1, 0].reshape(feat, hid), preferred_element_type=F32
    )
    dest_top = dest.astype(BF16)
    proj[0:rows] = dest_top
    proj[128:128 + rows] = (dest - dest_top.astype(F32)).astype(BF16)
    anchor = jnp.dot(window[2], weights[:, :, 0, 0].reshape(feat, hid), preferred_element_type=F32)
    anchor_top = anchor.astype(BF16)
    proj[rows:rows + blk] = anchor_top
    proj[128 + rows:128 + rows + blk] = (anchor - anchor_top.astype(F32)).astype(BF16)

    group = 4
    size = group * slots
    weight = w_out[...].astype(F32).reshape(1, hid)

    def score(i, scores):
        at = pl.multiple_of(i * size, size)
        pick = onehot[pl.ds(at, size), :]
        both = jnp.concatenate([pick, pick], axis=1)
        first = jnp.maximum(jnp.dot(both, proj[...], preferred_element_type=F32), 0.0).astype(BF16)
        first_t[:, pl.ds(at, size)] = first.T
        act = jnp.maximum(
            jnp.dot(first, weights[:, :, :, 1].reshape(hid, hid), preferred_element_type=F32), 0.0
        )
        active[pl.ds(at, size), :] = act
        col = jnp.sum(act * weight, axis=1, keepdims=True)
        for a in range(group):
            scores = jnp.where(lane16 == i * group + a, col[a * slots:(a + 1) * slots], scores)
        return scores

    scores = lax.fori_loop(0, blk // group, score, jnp.zeros((slots, blk), F32))

    top = jnp.max(jnp.where(valid, scores, -jnp.inf), axis=0, keepdims=True)
    expo = jnp.where(valid, jnp.exp(scores - top), 0.0)
    mass = jnp.sum(expo, axis=0, keepdims=True)
    probs = expo / mass
    logp = scores - top - jnp.log(mass)
    sgrad = jnp.where(valid, probs * anchor_total - flow, 0.0)
    numer = -jnp.sum(jnp.where(valid, flow * logp, 0.0))
    total = jnp.sum(anchor_total)

    def back(i, gout):
        at = pl.multiple_of(i * size, size)
        col = jnp.concatenate(
            [
                jnp.sum(jnp.where(lane16 == i * group + a, sgrad, 0.0), axis=1, keepdims=True)
                for a in range(group)
            ],
            axis=0,
        )
        act = active[pl.ds(at, size), :]
        pre[pl.ds(at, size), :] = jnp.where(act > 0, col * weight, 0.0).astype(BF16)
        return gout + jnp.sum((col * act).reshape(size // 8, 8, hid), axis=0)

    gout = lax.fori_loop(0, blk // group, back, jnp.zeros((8, hid), F32))
    gout = jnp.sum(gout, axis=0, keepdims=True)

    width = hid // 8
    for r in range(8):
        extra[r:r + 1, :] = gout[:, r * width:(r + 1) * width]
    row = lax.broadcasted_iota(jnp.int32, (8, width), 0)
    extra[8:16, :] = jnp.where(row == 0, numer, jnp.where(row == 1, total, 0.0))

    def extra_to_z(i):
        return remote(extra, extra_z.at[z], ez_send.at[i], ez_recv.at[i], at_z(wrap(z + i, depth)))

    def extra_from_z(i):
        where = wrap(z - i, depth)
        return remote(extra, extra_z.at[where], ez_send.at[i], ez_recv.at[i], at_z(where))

    def extra_to_plane(i):
        to = {"region": wrap(mine + i, planes)}
        return remote(extra_zsum, extra_plane.at[mine], ep_send.at[i], ep_recv.at[i], to)

    def extra_from_plane(i):
        p = wrap(mine - i, planes)
        return remote(extra_zsum, extra_plane.at[p], ep_send.at[i], ep_recv.at[i], {"region": p})

    each(1, depth, lambda i: extra_to_z(i).start())
    extra_z[z] = extra[...]

    wide = group_cols // 2
    turns = hid // wide

    def turn(n):
        return pl.ds(pl.multiple_of(n * wide, wide), wide)

    def to_sibling(n):
        return remote(
            grad.at[:, 1 - core, :, :, turn(n)], sib_grad.at[:, :, :, turn(n)], gs_send.at[n], gs_recv.at[n], sibling
        )

    def grads(n):
        part = jnp.dot(first_t[...], pre[:, turn(n)], preferred_element_type=F32)
        grad[:, :, :, :, turn(n)] = part.reshape(depth, 2, 2, 16, wide).astype(BF16)
        to_sibling(n).start()

    each(0, turns, grads)

    def to_u(n, h):
        uu = h * per_half + n // 2
        inside = pl.ds(pl.multiple_of((n % 2) * wide, wide), wide)
        return remote(
            chip_grad.at[:, h, :, turn(n)], u_in.at[u, :, :, inside],
            gu_send.at[n * 2 + h], gu_recv.at[u * 2 + n % 2], at_uv(uu, v),
        )

    def from_u_grad(uu, k):
        inside = pl.ds(pl.multiple_of(k * wide, wide), wide)
        return remote(
            chip_grad.at[:, 0, :, 0:wide], u_in.at[uu, :, :, inside],
            gu_send.at[0], gu_recv.at[uu * 2 + k], at_uv(uu, v),
        )

    def join(n):
        to_sibling(n).wait_recv()
        mine_part = grad[:, core, :, :, turn(n)].astype(F32)
        chip_grad[:, :, :, turn(n)] = (mine_part + sib_grad[:, :, :, turn(n)].astype(F32)).astype(BF16)
        for h in range(2):

            @pl.when(h * per_half + n // 2 != u)
            def _():
                to_u(n, h).start()

    each(0, turns, join)

    each(1, depth, lambda i: extra_from_z(i).wait_recv())
    extra_zsum[...] = jnp.sum(extra_z[...], axis=0)
    each(1, planes, lambda i: extra_to_plane(i).start())
    extra_plane[mine] = extra_zsum[...]

    def to_v(i):
        vv = wrap(v + i, side)
        part = u_sum.at[:, :, pl.ds(pl.multiple_of(vv * tile_cols, tile_cols), tile_cols)]
        return remote(part, v_in.at[v], gv_send.at[i], gv_recv.at[i], at_uv(u, vv))

    def from_v_grad(i):
        vv = wrap(v - i, side)
        part = u_sum.at[:, :, 0:tile_cols]
        return remote(part, v_in.at[vv], gv_send.at[i], gv_recv.at[i], at_uv(u, vv))

    for i in range(1, side):
        for k in range(2):
            from_u_grad(wrap(u + i, side), k).wait_recv()

    own_group = span(chip_grad, u, 0, side)

    def sum_u(i):
        acc = chip_grad[pl.ds(i * zs, zs), u // per_half, :, own_group].astype(F32)
        for k in range(1, side):
            acc = acc + u_in[wrap(u + k, side), pl.ds(i * zs, zs)].astype(F32)
        u_sum[pl.ds(i * zs, zs)] = acc.astype(BF16)

    each(0, 4, sum_u)
    for i in range(1, side):
        to_v(i).start()

    each(1, planes, lambda i: extra_from_plane(i).wait_recv())
    extra_psum[...] = jnp.sum(extra_plane[...], axis=0)
    extra_swap = remote(extra_psum, extra_sib, es_send, es_recv, sibling)
    extra_swap.start()

    def to_z(i):
        where = wrap(z + i, depth)
        return remote(plane_sum.at[where], z_in.at[z], gz_send.at[i], gz_recv.at[i], at_z(where))

    def from_z(i):
        where = wrap(z - i, depth)
        return remote(plane_sum.at[where], z_in.at[where], gz_send.at[i], gz_recv.at[i], at_z(where))

    for i in range(1, side):
        from_v_grad(i).wait_recv()
    own_cols = pl.ds(pl.multiple_of(v * tile_cols, tile_cols), tile_cols)
    acc = u_sum[:, :, own_cols].astype(F32)
    for k in range(1, side):
        acc = acc + v_in[wrap(v + k, side)].astype(F32)
    plane_sum[...] = acc.astype(BF16)
    each(1, depth, lambda i: to_z(i).start())
    z_in[z] = plane_sum[z]

    extra_swap.wait_recv()
    sums_all = extra_psum[...] + extra_sib[...]
    inverse = 1.0 / sums_all[9:10, :]
    gout_out[...] = sums_all[0:8, :] * inverse
    loss_out[...] = sums_all[8:9, 0:1] * inverse[:, 0:1]

    each(1, depth, lambda i: from_z(i).wait_recv())
    own_rows[...] = jnp.sum(z_in[...].astype(F32), axis=0) * inverse[0:1, 0:1]

    def out_tile(p):
        py, px = p // side, p % side
        uu = py + core * (px - py)
        vv = px + core * (py - px)
        return grad_out.at[pl.ds(pl.multiple_of((uu // per_half) * 16, 16), 16), span(grad_out, uu, vv, 1)]

    def share(i):
        to = {"region": wrap(mine + i, planes)}
        return remote(own_rows, out_tile(mine), ga_send.at[i], ga_recv.at[i], to)

    def shared(i):
        p = wrap(mine - i, planes)
        return remote(own_rows, out_tile(p), ga_send.at[i], ga_recv.at[i], {"region": p})

    each(1, planes, lambda i: share(i).start())
    own_out = pltpu.make_async_copy(own_rows, out_tile(mine), local_sem.at[1])
    own_out.start()

    for by in (-2, -1, 1, 2):
        halo(by).wait_send()
    each(1, depth, lambda i: to_z_weights(i).wait_send())

    def weights_left(b):
        for i in range(1, side):
            along_v(b, i).wait_send()
            along_u(b, i).wait_send()
        for i in range(side):
            hand(b, i).wait_send()

    each(0, 4, weights_left)
    each(1, depth, lambda i: extra_to_z(i).wait_send())
    each(1, planes, lambda i: extra_to_plane(i).wait_send())
    extra_swap.wait_send()
    each(0, turns, lambda n: to_sibling(n).wait_send())

    def u_left(n):
        for h in range(2):

            @pl.when(h * per_half + n // 2 != u)
            def _():
                to_u(n, h).wait_send()

    each(0, turns, u_left)
    for i in range(1, side):
        to_v(i).wait_send()
    each(1, depth, lambda i: to_z(i).wait_send())
    own_out.wait()
    each(1, planes, lambda i: shared(i).wait_recv())
    each(1, planes, lambda i: share(i).wait_send())


def shards(tiles, tile_block, neighbors, counts, flows, w_anchor, w_dest, w_hidden, w_out):
    planes, shard_count = lax.axis_size("region"), lax.axis_size("shard")
    side = 4 if planes == 16 else 2
    depth = shard_count // 2
    blk, slots = neighbors.shape
    feat, hid = tiles.shape[1], w_hidden.shape[1]
    pairs = blk * slots
    group_cols = hid // (side // 2)
    tile_cols = group_cols // side
    turns = hid // (group_cols // 2)
    width = hid // 8
    vmem = pl.BlockSpec(memory_space=pltpu.VMEM)
    hbm = pl.BlockSpec(memory_space=pltpu.HBM)
    dma = lambda n: pltpu.SemaphoreType.DMA((n,))
    scratch = [
        pltpu.VMEM(tiles.shape, BF16),
        pltpu.VMEM((1, tile_block.shape[0]), jnp.int32),
        pltpu.VMEM((blk, slots), jnp.int32),
        pltpu.SMEM((blk,), jnp.int32),
        pltpu.VMEM((blk, slots), jnp.int32),
        pltpu.VMEM((hid,), BF16),
        pltpu.VMEM((2, 2, 16, hid), BF16),
        pltpu.VMEM((depth, 2, 2, 2, 16, hid), BF16),
        pltpu.VMEM((5, blk, feat), BF16),
        pltpu.VMEM((256, hid), BF16),
        pltpu.VMEM((pairs, 128), BF16),
        pltpu.VMEM((hid, pairs), BF16),
        pltpu.VMEM((pairs, hid), F32),
        pltpu.VMEM((pairs, hid), BF16),
        pltpu.VMEM((depth, 2, 2, 16, hid), BF16),
        pltpu.VMEM((depth, 2, 16, hid), BF16),
        pltpu.VMEM((depth, 2, 16, hid), BF16),
        pltpu.VMEM((side, depth, 16, group_cols), BF16),
        pltpu.VMEM((depth, 16, group_cols), BF16),
        pltpu.VMEM((side, depth, 16, tile_cols), BF16),
        pltpu.VMEM((depth, 16, tile_cols), BF16),
        pltpu.VMEM((depth, 16, tile_cols), BF16),
        pltpu.VMEM((16, tile_cols), F32),
        pltpu.VMEM((16, width), F32),
        pltpu.VMEM((depth, 16, width), F32),
        pltpu.VMEM((16, width), F32),
        pltpu.VMEM((planes, 16, width), F32),
        pltpu.VMEM((16, width), F32),
        pltpu.VMEM((16, width), F32),
        dma(5), dma(5), dma(depth), dma(depth), dma(4 * side), dma(4 * side), dma(4 * side), dma(4 * side),
        dma(4 * side), dma(4 * side), dma(turns), dma(turns), dma(2 * turns), dma(2 * side), dma(side), dma(side),
        dma(depth), dma(depth), dma(planes), dma(planes), dma(depth), dma(depth), dma(planes), dma(planes),
        pltpu.SemaphoreType.DMA, pltpu.SemaphoreType.DMA, dma(10), dma(2),
    ]
    grad, gout, loss = pl.pallas_call(
        functools.partial(step_kernel, (side, depth, blk, slots, hid)),
        out_shape=(
            jax.ShapeDtypeStruct((w_hidden.shape[0], hid), F32),
            jax.ShapeDtypeStruct((8, width), F32),
            jax.ShapeDtypeStruct((1, 1), F32),
        ),
        in_specs=[hbm] * 9,
        out_specs=(vmem, vmem, vmem),
        scratch_shapes=scratch,
        compiler_params=pltpu.CompilerParams(
            collective_id=0, has_side_effects=True, vmem_limit_bytes=62 * 2 ** 20
        ),
        cost_estimate=pl.CostEstimate(
            flops=4 * pairs * hid * hid, bytes_accessed=2 * tiles.size, transcendentals=pairs
        ),
    )(tiles, tile_block.reshape(1, -1), neighbors, counts, flows, w_anchor, w_dest, w_hidden, w_out)
    return grad, gout.reshape(hid), loss.reshape(())


def solution(mesh):
    return jax.shard_map(
        shards,
        mesh=mesh,
        in_specs=(
            P(("region", "shard"), None),
            P(("region", "shard")),
            P(("region", "shard"), None),
            P(("region", "shard")),
            P(("region", "shard"), None),
            P("shard", None),
            P("shard", None),
            P("shard", None),
            P(),
        ),
        out_specs=(P("shard", None), P(), P()),
        check_vma=False,
    )
```

time: 574 us -> 91.2 us (0.16)
  waiting for transfers between devices: 301 us -> 0 us
  blocking collectives: 209 us -> 0 us
  Pallas kernels: 0 us -> 86.1 us
  matrix products: 16.7 us -> 0 us
  between operations: 17 us -> 2.41 us
  starting transfers between devices: 12.9 us -> 0 us
  other arithmetic: 8.82 us -> 0 us
    psum x2 -> x0, blocking collectives: 209 us -> none  [the longest x1 106 us: shards(): numer_all, out_grad = lax.psum((numer, gout), ('region', 'shard'))]
    all_gather x3 -> x0, waiting for transfers between devices: 190 us -> none  [the longest x1 66.8 us: shards(): lax.all_gather(w_hidden, 'shard', axis=0, tiled=True)]
    reduce_scatter x1 -> x0, waiting for transfers between devices: 104 us -> none  [shards(): lax.psum_scatter(grad, 'shard', scatter_dimension=0, tiled=True)]
    pallas_call x0 -> x1, Pallas kernels: none -> 86.1 us  [shards(): pl.pallas_call(functools.partial(step_kernel, (side, depth, blk, slots, h...]
    dot_general x5 -> x0, matrix products: 16.7 us -> none  [the longest x1 6.74 us: shards(): lax.dot_general(first, pre, (((0,), (0,)), ((), ())), preferred_element_t...]
    ppermute x4 -> x0, starting transfers between devices: 12.7 us -> none  [shifted(): return lax.ppermute(array, axis, pairs)]
  transfers between devices with their start and end apart: 9 -> 0, of which waited for: 6 -> 0; matrix products, arithmetic and copies ran while one was open for 3% -> 0% of each run, Pallas kernels for 0% -> 0%
where the time goes in v2:
time: 91.2 us; the launch traced here: 90.6 us
  Pallas kernels  86.1 us (94%)
  between operations  2.41 us (3%)
  local copies, waits for them, and re-layouts  2.17 us (2%)
    pallas_call x1, Pallas kernels, shards(): pl.pallas_call(functools.partial(step_kernel, (side, depth, blk, slots, h...  86.1 us
    unnamed x4, local copies, waits for them, and re-layouts  2.17 us

profile of v2, /device:TPU:1, one launch (start us, length us, event | category | flops | bytes accessed | tf_op | source)
XLA Modules:
  0.0 90.6 jit_solution(310880491793946397)
XLA Ops:
  0.6 86.1 %shard_map.112 = (f32[32,1024]{1,0:T(8,128)}, f32[8,128]{1,0:T(8,128)}, f32[1,1]{1,0:T(1,128)}) custom-call(bf16[1024,512]{1,0:T(8,128)(2,1)} %tiles_hbm.1, s32[1,1024]{1,0:T(1,128)} %bitcast.4, s32[16,64]{1,0:T(8,128)} %neighbors_hbm.1, s32[16]{0:T(128)} %counts_hbm.1, s32[16,64]{1,0:T(8,128)} %flows_hbm.1, bf16[16,1024]{1,0:T(8,128)(2,1)} %anchor_hbm.1, ...), custom_call_target="tpu_custom_call" | custom-call | flops 4294967296 | bytes 1048576 | tf_op jit(solution)/shard_map/pallas_call | solution.py:510
  86.7 0.0 copy-start
  86.7 1.6 %copy.15 = f32[32,1024]{1,0:T(8,128)} copy(f32[32,1024]{1,0:T(8,128)} %get-tuple-element.12) | data formatting | bytes 262144
  88.3 0.0 copy-done
  88.3 0.6 copy.16
Async XLA Ops:
  86.7 1.6 %copy-start = (f32[8,128]{1,0:T(8,128)S(1)}, f32[8,128]{1,0:T(8,128)}, u32[]{:S(2)}) copy-start(f32[8,128]{1,0:T(8,128)} %get-tuple-element.7) | copy-start | bytes 12292

commit v3 on v2

--- a/solution.py
+++ b/solution.py
@@ -23,9 +23,10 @@
     tiles_hbm, tile_block_hbm, neighbors_hbm, counts_hbm, flows_hbm, anchor_hbm, dest_hbm, hidden_hbm, out_hbm,
     grad_out, gout_out, loss_out,
     tiles, tile_block, neighbors, counts, flows, w_out,
-    own_w, weights, window, proj, onehot, first_t, active, pre, grad, sib_grad, chip_grad, u_in, u_sum, v_in,
+    weights, features, tile_w, plane_feats, part_proj, own_proj, window, proj, onehot, first_t, active, pre, grad, sib_grad, chip_grad, u_in, u_sum, v_in,
     plane_sum, z_in, own_rows, extra, extra_z, extra_zsum, extra_plane, extra_psum, extra_sib,
-    halo_send, halo_recv, az_send, az_recv, p1_send, p1_recv, p2_send, p2_recv, sb_send, sb_recv,
+    halo_send, halo_recv, fz_send, fz_recv, fs_send, fs_recv, fp_send, fp_recv, pp_send, pp_recv,
+    az_send, az_recv, p1_send, p1_recv, p2_send, p2_recv, sb_send, sb_recv,
     gs_send, gs_recv, gu_send, gu_recv, gv_send, gv_recv, gz_send, gz_recv,
     ga_send, ga_recv, ez_send, ez_recv, ep_send, ep_recv, es_send, es_recv, load_sem, local_sem,
 ):
@@ -63,19 +64,13 @@
         lax.fori_loop(first, last, body, 0)
 
     loads = [
-        pltpu.make_async_copy(anchor_hbm, own_w.at[0, 0], load_sem.at[0]),
-        pltpu.make_async_copy(dest_hbm, own_w.at[1, 0], load_sem.at[1]),
-        pltpu.make_async_copy(hidden_hbm.at[0:16], own_w.at[0, 1], load_sem.at[2]),
-        pltpu.make_async_copy(hidden_hbm.at[16:32], own_w.at[1, 1], load_sem.at[3]),
-        pltpu.make_async_copy(tiles_hbm, tiles, load_sem.at[4]),
-        pltpu.make_async_copy(tile_block_hbm, tile_block, load_sem.at[5]),
-        pltpu.make_async_copy(neighbors_hbm, neighbors, load_sem.at[6]),
-        pltpu.make_async_copy(counts_hbm, counts, load_sem.at[7]),
-        pltpu.make_async_copy(flows_hbm, flows, load_sem.at[8]),
-        pltpu.make_async_copy(out_hbm, w_out, load_sem.at[9]),
+        pltpu.make_async_copy(tiles_hbm, tiles, load_sem.at[0]),
+        pltpu.make_async_copy(tile_block_hbm, tile_block, load_sem.at[1]),
+        pltpu.make_async_copy(neighbors_hbm, neighbors, load_sem.at[2]),
+        pltpu.make_async_copy(counts_hbm, counts, load_sem.at[3]),
+        pltpu.make_async_copy(flows_hbm, flows, load_sem.at[4]),
+        pltpu.make_async_copy(out_hbm, w_out, load_sem.at[5]),
     ]
-    for copy in loads:
-        copy.start()
     barrier = pltpu.get_barrier_semaphore()
 
     def greet(where):
@@ -86,58 +81,84 @@
     each(1, depth, lambda i: greet(at_z(wrap(z + i, depth))))
     each(1, planes, lambda i: greet({"region": wrap(mine + i, planes)}))
 
-    def span(ref, uu, first, count):
+    for copy in loads:
+        copy.start()
+
+    def span(uu, first, count):
         at = (uu % per_half) * group_cols + first * tile_cols
         return pl.ds(pl.multiple_of(at, tile_cols), count * tile_cols)
 
-    def weight_tile(where, zs):
-        return weights.at[pl.ds(where, zs), core, u // per_half, :, :, span(weights, u, v, 1)]
-
-    def weight_group(where, zs, uu, cc):
-        return weights.at[pl.ds(where, zs), cc, uu // per_half, :, :, span(weights, uu, 0, side)]
-
-    own_tile = own_w.at[u // per_half, :, :, span(own_w, u, v, 1)]
+    def weight_part(where, count, cc, uu, first, tiles_of):
+        return weights.at[pl.ds(where, count), cc, uu // per_half, :, span(uu, first, tiles_of)]
+
+    half_planes = planes // 2
+    matrix = mine // half_planes
+    first_cols = pl.ds(pl.multiple_of((mine % half_planes) * tile_cols, tile_cols), tile_cols)
+    hid_tile = hidden_hbm.at[pl.ds(pl.multiple_of((u // per_half) * 16, 16), 16), span(u, v, 1)]
 
     def weight_slot(where):
-        return weights.at[where, core, u // per_half, :, :, span(weights, u, v, 1)]
-
-    def to_z_weights(i):
+        return weights.at[where, core, u // per_half, :, span(u, v, 1)]
+
+    def first_to_z(i, source):
         to = wrap(z + i, depth)
-        return remote(own_tile, weight_slot(z), az_send.at[to], az_recv.at[z], at_z(to))
-
-    def from_z_weights(where):
-        return remote(own_tile, weight_slot(where), az_send.at[where], az_recv.at[where], at_z(where))
-
-    for copy in loads[0:4]:
-        copy.wait()
-    keep_tile = pltpu.make_async_copy(own_tile, weight_slot(z), local_sem.at[0])
+        return remote(source.at[:, first_cols], tile_w.at[z, core], fz_send.at[to], fz_recv.at[z], at_z(to))
+
+    def first_from_z(where):
+        return remote(
+            anchor_hbm.at[:, first_cols], tile_w.at[where, core], fz_send.at[where], fz_recv.at[where], at_z(where)
+        )
+
+    def hid_to_z(i):
+        to = wrap(z + i, depth)
+        return remote(hid_tile, weight_slot(z), az_send.at[to], az_recv.at[z], at_z(to))
+
+    def hid_from_z(where):
+        return remote(hid_tile, weight_slot(where), az_send.at[where], az_recv.at[where], at_z(where))
+
+    def keep_first(source):
+        return pltpu.make_async_copy(source.at[:, first_cols], tile_w.at[z, core], local_sem.at[2])
+
+    def near_first(start):
+        def both_ways(i):
+            start(i)
+            start(depth - i)
+
+        each(1, depth // 2, both_ways)
+        start(depth // 2)
+
+    pl.semaphore_wait(barrier, planes - 1 + depth - 1 + 2)
+    for k, source in enumerate((anchor_hbm, dest_hbm)):
+
+        @pl.when(matrix == k)
+        def _():
+            near_first(lambda i: first_to_z(i, source).start())
+            keep_first(source).start()
+
+    near_first(lambda i: hid_to_z(i).start())
+    keep_tile = pltpu.make_async_copy(hid_tile, weight_slot(z), local_sem.at[0])
     keep_tile.start()
-    pl.semaphore_wait(barrier, planes - 1 + depth - 1 + 2)
-
-    def both_ways(i):
-        to_z_weights(i).start()
-        to_z_weights(depth - i).start()
-
-    each(1, depth // 2, both_ways)
-    to_z_weights(depth // 2).start()
-
-    for copy in loads[4:]:
-        copy.wait()
+
+    loads[0].wait()
+    loads[1].wait()
     member = tile_block[...] == lax.broadcasted_iota(jnp.int32, (blk, tile_block.shape[1]), 0)
     sums = jnp.dot(member.astype(BF16), tiles[...], preferred_element_type=F32)
     scale = lax.rsqrt(jnp.mean(sums * sums, axis=-1, keepdims=True) + 1e-05)
-    window[2] = (sums * scale).astype(BF16)
-
-    def halo(by):
-        return remote(
-            window.at[2], window.at[2 - by], halo_send.at[by + 2], halo_recv.at[by + 2],
-            {"shard": wrap(pos + by, shards)},
-        )
-
-    for by in (-2, -1, 1, 2):
-        halo(by).start()
+    features[...] = (sums * scale).astype(BF16)
+    plane_feats[mine] = features[...]
+
+    def feats_to(i):
+        p = wrap(mine + i, planes)
+        return remote(features, plane_feats.at[mine], fp_send.at[i], fp_recv.at[i], {"region": p})
+
+    def feats_from(i):
+        p = wrap(mine - i, planes)
+        return remote(features, plane_feats.at[p], fp_send.at[i], fp_recv.at[i], {"region": p})
+
+    each(1, planes, lambda i: feats_to(i).start())
 
     shift = mine * (blk * shards) + (pos - 2) * blk
+    for copy in loads[2:]:
+        copy.wait()
     place = (neighbors[...] - shift).astype(F32).T
     flow = flows[...].astype(F32).T
     lane16 = lax.broadcasted_iota(jnp.int32, (slots, blk), 1)
@@ -153,6 +174,8 @@
     proj[...] = jnp.zeros_like(proj)
     keep_tile.wait()
 
+    keep_first(anchor_hbm).wait()
+
     zs = depth // 4
     first_block = z // zs
 
@@ -160,74 +183,139 @@
         return wrap(first_block + (0, 1, -1, 2)[n], 4)
 
     def along_v(b, i):
-        tile = weight_tile(b * zs, zs)
+        tile = weight_part(b * zs, zs, core, u, v, 1)
         return remote(
             tile, tile, p1_send.at[b * side + i], p1_recv.at[b * side + i], at_uv(u, wrap(v + i, side))
         )
 
     def from_v(b, i):
         vv = wrap(v - i, side)
-        tile = weights.at[pl.ds(b * zs, zs), core, u // per_half, :, :, span(weights, u, vv, 1)]
+        tile = weight_part(b * zs, zs, core, u, vv, 1)
         return remote(tile, tile, p1_send.at[b * side + i], p1_recv.at[b * side + i], at_uv(u, vv))
 
     def along_u(b, i):
-        part = weight_group(b * zs, zs, u, core)
+        part = weight_part(b * zs, zs, core, u, 0, side)
         return remote(
             part, part, p2_send.at[b * side + i], p2_recv.at[b * side + i], at_uv(wrap(u + i, side), v)
         )
 
     def from_u(b, i):
         uu = wrap(u - i, side)
-        part = weight_group(b * zs, zs, uu, core)
+        part = weight_part(b * zs, zs, core, uu, 0, side)
         return remote(part, part, p2_send.at[b * side + i], p2_recv.at[b * side + i], at_uv(uu, v))
 
     def hand(b, i):
-        part = weight_group(b * zs, zs, wrap(u - i, side), core)
+        part = weight_part(b * zs, zs, core, wrap(u - i, side), 0, side)
         return remote(part, part, sb_send.at[b * side + i], sb_recv.at[b * side + i], sibling)
 
     def take(b, i):
-        part = weight_group(b * zs, zs, wrap(v - i, side), 1 - core)
+        part = weight_part(b * zs, zs, 1 - core, wrap(v - i, side), 0, side)
         return remote(part, part, sb_send.at[b * side + i], sb_recv.at[b * side + i], sibling)
 
-    for n in range(6):
-        if 1 <= n <= 4:
-            b = block_at(n - 1)
-            for i in range(1, side):
-                from_v(b, i).wait_recv()
-            for i in range(1, side):
-                along_u(b, i).start()
-            hand(b, 0).start()
-        if n < 4:
-            b = block_at(n)
-            for k in range(zs):
-
-                @pl.when(b * zs + k != z)
-                def _():
-                    from_z_weights(b * zs + k).wait_recv()
-
-            for i in range(1, side):
-                along_v(b, i).start()
-        if n >= 2:
-            b = block_at(n - 2)
-            for i in range(1, side):
-                from_u(b, i).wait_recv()
-                hand(b, i).start()
-
+    def hand_first(b, cc):
+        part = tile_w.at[pl.ds(b * zs, zs), cc]
+        return remote(part, part, fs_send.at[b], fs_recv.at[b], sibling)
+
+    def first_block_in(n):
+        b = block_at(n)
+        for k in range(zs):
+
+            @pl.when(b * zs + k != z)
+            def _():
+                first_from_z(b * zs + k).wait_recv()
+
+        hand_first(b, core).start()
+
+    def hid_block_in(n):
+        b = block_at(n)
+        for k in range(zs):
+
+            @pl.when(b * zs + k != z)
+            def _():
+                hid_from_z(b * zs + k).wait_recv()
+
+        for i in range(1, side):
+            along_v(b, i).start()
+
+    def v_in_block(n):
+        b = block_at(n)
+        for i in range(1, side):
+            from_v(b, i).wait_recv()
+        for i in range(1, side):
+            along_u(b, i).start()
+        hand(b, 0).start()
+
+    def u_in_block(n):
+        b = block_at(n)
+        for i in range(1, side):
+            from_u(b, i).wait_recv()
+            hand(b, i).start()
+
+    first_block_in(0)
+    hid_block_in(0)
+    first_block_in(1)
+    first_block_in(2)
+    first_block_in(3)
+    v_in_block(0)
+
+    each(1, planes, lambda i: feats_from(i).wait_recv())
+    each(0, 4, lambda b: hand_first(b, 1 - core).wait_recv())
+    part_proj[...] = jnp.dot(
+        plane_feats[...].reshape(planes * blk, feat), tile_w[...].reshape(feat, tile_cols),
+        preferred_element_type=F32,
+    ).reshape(planes, blk, tile_cols)
+
+    def proj_tile(p):
+        at = pl.multiple_of((p % half_planes) * tile_cols, tile_cols)
+        return own_proj.at[p // half_planes, :, pl.ds(at, tile_cols)]
+
+    def proj_to(i):
+        p = wrap(mine + i, planes)
+        return remote(part_proj.at[p], proj_tile(mine), pp_send.at[i], pp_recv.at[i], {"region": p})
+
+    def proj_from(i):
+        p = wrap(mine - i, planes)
+        return remote(part_proj.at[p], proj_tile(p), pp_send.at[i], pp_recv.at[i], {"region": p})
+
+    each(1, planes, lambda i: proj_to(i).start())
+    keep_proj = pltpu.make_async_copy(part_proj.at[mine], proj_tile(mine), local_sem.at[3])
+    keep_proj.start()
+
+    hid_block_in(1)
+    hid_block_in(2)
+    v_in_block(1)
+    hid_block_in(3)
+    v_in_block(2)
+    u_in_block(0)
+    keep_proj.wait()
+    each(1, planes, lambda i: proj_from(i).wait_recv())
+
+    def halo(by):
+        return remote(
+            own_proj.at[1], window.at[2 - by], halo_send.at[by + 2], halo_recv.at[by + 2],
+            {"shard": wrap(pos + by, shards)},
+        )
+
+    for by in (-2, -1, 1, 2):
+        halo(by).start()
+    window[2] = own_proj[1]
+    v_in_block(3)
+    u_in_block(1)
+    u_in_block(2)
+    u_in_block(3)
     for by in (-2, -1, 1, 2):
         halo(by).wait_recv()
-    each(0, 4 * side, lambda i: take(i // side, i % side).wait_recv())
 
     rows = 5 * blk
-    dest = jnp.dot(
-        window[...].reshape(rows, feat), weights[:, :, 1, 0].reshape(feat, hid), preferred_element_type=F32
-    )
+    dest = window[...].reshape(rows, hid)
     dest_top = dest.astype(BF16)
     proj[0:rows] = dest_top
     proj[128:128 + rows] = (dest - dest_top.astype(F32)).astype(BF16)
-    anchor = jnp.dot(window[2], weights[:, :, 0, 0].reshape(feat, hid), preferred_element_type=F32)
+    anchor = own_proj[0]
     anchor_top = anchor.astype(BF16)
     proj[rows:rows + blk] = anchor_top
     proj[128 + rows:128 + rows + blk] = (anchor - anchor_top.astype(F32)).astype(BF16)
+    each(0, 4 * side, lambda i: take(i // side, i % side).wait_recv())
 
     group = 4
     size = group * slots
@@ -240,7 +328,7 @@
         first = jnp.maximum(jnp.dot(both, proj[...], preferred_element_type=F32), 0.0).astype(BF16)
         first_t[:, pl.ds(at, size)] = first.T
         act = jnp.maximum(
-            jnp.dot(first, weights[:, :, :, 1].reshape(hid, hid), preferred_element_type=F32), 0.0
+            jnp.dot(first, weights[...].reshape(hid, hid), preferred_element_type=F32), 0.0
         )
         active[pl.ds(at, size), :] = act
         col = jnp.sum(act * weight, axis=1, keepdims=True)
@@ -344,11 +432,6 @@
 
     each(0, turns, join)
 
-    each(1, depth, lambda i: extra_from_z(i).wait_recv())
-    extra_zsum[...] = jnp.sum(extra_z[...], axis=0)
-    each(1, planes, lambda i: extra_to_plane(i).start())
-    extra_plane[mine] = extra_zsum[...]
-
     def to_v(i):
         vv = wrap(v + i, side)
         part = u_sum.at[:, :, pl.ds(pl.multiple_of(vv * tile_cols, tile_cols), tile_cols)]
@@ -363,7 +446,7 @@
         for k in range(2):
             from_u_grad(wrap(u + i, side), k).wait_recv()
 
-    own_group = span(chip_grad, u, 0, side)
+    own_group = span(u, 0, side)
 
     def sum_u(i):
         acc = chip_grad[pl.ds(i * zs, zs), u // per_half, :, own_group].astype(F32)
@@ -375,10 +458,10 @@
     for i in range(1, side):
         to_v(i).start()
 
-    each(1, planes, lambda i: extra_from_plane(i).wait_recv())
-    extra_psum[...] = jnp.sum(extra_plane[...], axis=0)
-    extra_swap = remote(extra_psum, extra_sib, es_send, es_recv, sibling)
-    extra_swap.start()
+    each(1, depth, lambda i: extra_from_z(i).wait_recv())
+    extra_zsum[...] = jnp.sum(extra_z[...], axis=0)
+    each(1, planes, lambda i: extra_to_plane(i).start())
+    extra_plane[mine] = extra_zsum[...]
 
     def to_z(i):
         where = wrap(z + i, depth)
@@ -398,6 +481,10 @@
     each(1, depth, lambda i: to_z(i).start())
     z_in[z] = plane_sum[z]
 
+    each(1, planes, lambda i: extra_from_plane(i).wait_recv())
+    extra_psum[...] = jnp.sum(extra_plane[...], axis=0)
+    extra_swap = remote(extra_psum, extra_sib, es_send, es_recv, sibling)
+    extra_swap.start()
     extra_swap.wait_recv()
     sums_all = extra_psum[...] + extra_sib[...]
     inverse = 1.0 / sums_all[9:10, :]
@@ -411,7 +498,7 @@
         py, px = p // side, p % side
         uu = py + core * (px - py)
         vv = px + core * (py - px)
-        return grad_out.at[pl.ds(pl.multiple_of((uu // per_half) * 16, 16), 16), span(grad_out, uu, vv, 1)]
+        return grad_out.at[pl.ds(pl.multiple_of((uu // per_half) * 16, 16), 16), span(uu, vv, 1)]
 
     def share(i):
         to = {"region": wrap(mine + i, planes)}
@@ -427,7 +514,11 @@
 
     for by in (-2, -1, 1, 2):
         halo(by).wait_send()
-    each(1, depth, lambda i: to_z_weights(i).wait_send())
+    each(1, depth, lambda i: first_to_z(i, anchor_hbm).wait_send())
+    each(1, depth, lambda i: hid_to_z(i).wait_send())
+    each(0, 4, lambda b: hand_first(b, core).wait_send())
+    each(1, planes, lambda i: feats_to(i).wait_send())
+    each(1, planes, lambda i: proj_to(i).wait_send())
 
     def weights_left(b):
         for i in range(1, side):
@@ -479,9 +570,13 @@
         pltpu.SMEM((blk,), jnp.int32),
         pltpu.VMEM((blk, slots), jnp.int32),
         pltpu.VMEM((hid,), BF16),
-        pltpu.VMEM((2, 2, 16, hid), BF16),
-        pltpu.VMEM((depth, 2, 2, 2, 16, hid), BF16),
-        pltpu.VMEM((5, blk, feat), BF16),
+        pltpu.VMEM((depth, 2, 2, 16, hid), BF16),
+        pltpu.VMEM((blk, feat), BF16),
+        pltpu.VMEM((depth, 2, 16, tile_cols), BF16),
+        pltpu.VMEM((planes, blk, feat), BF16),
+        pltpu.VMEM((planes, blk, tile_cols), F32),
+        pltpu.VMEM((2, blk, hid), F32),
+        pltpu.VMEM((5, blk, hid), F32),
         pltpu.VMEM((256, hid), BF16),
         pltpu.VMEM((pairs, 128), BF16),
         pltpu.VMEM((hid, pairs), BF16),
@@ -502,10 +597,11 @@
         pltpu.VMEM((planes, 16, width), F32),
         pltpu.VMEM((16, width), F32),
         pltpu.VMEM((16, width), F32),
-        dma(5), dma(5), dma(depth), dma(depth), dma(4 * side), dma(4 * side), dma(4 * side), dma(4 * side),
+        dma(5), dma(5), dma(depth), dma(depth), dma(4), dma(4), dma(planes), dma(planes), dma(planes), dma(planes),
+        dma(depth), dma(depth), dma(4 * side), dma(4 * side), dma(4 * side), dma(4 * side),
         dma(4 * side), dma(4 * side), dma(turns), dma(turns), dma(2 * turns), dma(2 * side), dma(side), dma(side),
         dma(depth), dma(depth), dma(planes), dma(planes), dma(depth), dma(depth), dma(planes), dma(planes),
-        pltpu.SemaphoreType.DMA, pltpu.SemaphoreType.DMA, dma(10), dma(2),
+        pltpu.SemaphoreType.DMA, pltpu.SemaphoreType.DMA, dma(6), dma(4),
     ]
     grad, gout, loss = pl.pallas_call(
         functools.partial(step_kernel, (side, depth, blk, slots, hid)),

time: 91.2 us -> 86.2 us (0.945); the launches traced: 90.6 us -> 84.7 us
  Pallas kernels: 86.1 us -> 80.1 us
    pallas_call x1, Pallas kernels: 86.1 us -> 80.1 us  [shards(): pl.pallas_call(functools.partial(step_kernel, (side, depth, blk, slots, h...]
where the time goes in v3:
time: 86.2 us; the launch traced here: 84.7 us
  Pallas kernels  80.1 us (93%)
  between operations  2.41 us (3%)
  local copies, waits for them, and re-layouts  2.17 us (3%)
    pallas_call x1, Pallas kernels, shards(): pl.pallas_call(functools.partial(step_kernel, (side, depth, blk, slots, h...  80.1 us
    unnamed x4, local copies, waits for them, and re-layouts  2.17 us

profile of v3, /device:TPU:1, one launch (start us, length us, event | category | flops | bytes accessed | tf_op | source)
XLA Modules:
  0.0 84.7 jit_solution(12686440664993128731)
XLA Ops:
  0.6 80.1 %shard_map.112 = (f32[32,1024]{1,0:T(8,128)}, f32[8,128]{1,0:T(8,128)}, f32[1,1]{1,0:T(1,128)}) custom-call(bf16[1024,512]{1,0:T(8,128)(2,1)} %tiles_hbm.1, s32[1,1024]{1,0:T(1,128)} %bitcast.4, s32[16,64]{1,0:T(8,128)} %neighbors_hbm.1, s32[16]{0:T(128)} %counts_hbm.1, s32[16,64]{1,0:T(8,128)} %flows_hbm.1, bf16[16,1024]{1,0:T(8,128)(2,1)} %anchor_hbm.1, ...), custom_call_target="tpu_custom_call" | custom-call | flops 4294967296 | bytes 1048576 | tf_op jit(solution)/shard_map/pallas_call | solution.py:606
  80.8 0.0 copy-start
  80.8 1.6 %copy.15 = f32[32,1024]{1,0:T(8,128)} copy(f32[32,1024]{1,0:T(8,128)} %get-tuple-element.12) | data formatting | bytes 262144
  82.3 0.0 copy-done
  82.3 0.6 copy.16
Async XLA Ops:
  80.8 1.6 %copy-start = (f32[8,128]{1,0:T(8,128)S(1)}, f32[8,128]{1,0:T(8,128)}, u32[]{:S(2)}) copy-start(f32[8,128]{1,0:T(8,128)} %get-tuple-element.7) | copy-start | bytes 12292

commit v4 on v3

--- a/solution.py
+++ b/solution.py
@@ -16,6 +16,14 @@
     return pltpu.make_async_remote_copy(
         src_ref=src, dst_ref=dst, send_sem=send, recv_sem=recv, device_id=where, device_id_type=MESH
     )
+
+
+def arrived(ref, sem, where):
+    remote(ref, ref, sem, sem, where).wait_recv()
+
+
+def left(ref, sem, where):
+    remote(ref, ref, sem, sem, where).wait_send()
 
 
 def step_kernel(
@@ -76,11 +84,15 @@
     def greet(where):
         pl.semaphore_signal(barrier, inc=1, device_id=where, device_id_type=MESH)
 
+    def greet_z(i):
+        greet(at_z(wrap(z + depth // 2 + i, depth)))
+        greet(at_z(wrap(z + depth // 2 - i, depth)))
+
+    greet(at_z(wrap(z + depth // 2, depth)))
+    each(1, depth // 2, greet_z)
+    each(1, planes, lambda i: greet({"region": wrap(mine + i, planes)}))
+    greet(cross)
     greet(sibling)
-    greet(cross)
-    each(1, depth, lambda i: greet(at_z(wrap(z + i, depth))))
-    each(1, planes, lambda i: greet({"region": wrap(mine + i, planes)}))
-
     for copy in loads:
         copy.start()
 
@@ -99,21 +111,16 @@
     def weight_slot(where):
         return weights.at[where, core, u // per_half, :, span(u, v, 1)]
 
+    zs = depth // 4
+    first_block = z // zs
+
     def first_to_z(i, source):
-        to = wrap(z + i, depth)
-        return remote(source.at[:, first_cols], tile_w.at[z, core], fz_send.at[to], fz_recv.at[z], at_z(to))
-
-    def first_from_z(where):
-        return remote(
-            anchor_hbm.at[:, first_cols], tile_w.at[where, core], fz_send.at[where], fz_recv.at[where], at_z(where)
-        )
+        to = at_z(wrap(z + i, depth))
+        return remote(source.at[:, first_cols], tile_w.at[z, core], fz_send, fz_recv.at[first_block], to)
 
     def hid_to_z(i):
-        to = wrap(z + i, depth)
-        return remote(hid_tile, weight_slot(z), az_send.at[to], az_recv.at[z], at_z(to))
-
-    def hid_from_z(where):
-        return remote(hid_tile, weight_slot(where), az_send.at[where], az_recv.at[where], at_z(where))
+        to = at_z(wrap(z + i, depth))
+        return remote(hid_tile, weight_slot(z), az_send, az_recv.at[first_block], to)
 
     def keep_first(source):
         return pltpu.make_async_copy(source.at[:, first_cols], tile_w.at[z, core], local_sem.at[2])
@@ -148,11 +155,7 @@
 
     def feats_to(i):
         p = wrap(mine + i, planes)
-        return remote(features, plane_feats.at[mine], fp_send.at[i], fp_recv.at[i], {"region": p})
-
-    def feats_from(i):
-        p = wrap(mine - i, planes)
-        return remote(features, plane_feats.at[p], fp_send.at[i], fp_recv.at[i], {"region": p})
+        return remote(features, plane_feats.at[mine], fp_send, fp_recv, {"region": p})
 
     each(1, planes, lambda i: feats_to(i).start())
 
@@ -176,71 +179,52 @@
 
     keep_first(anchor_hbm).wait()
 
-    zs = depth // 4
-    first_block = z // zs
-
     def block_at(n):
         return wrap(first_block + (0, 1, -1, 2)[n], 4)
 
     def along_v(b, i):
         tile = weight_part(b * zs, zs, core, u, v, 1)
         return remote(
-            tile, tile, p1_send.at[b * side + i], p1_recv.at[b * side + i], at_uv(u, wrap(v + i, side))
-        )
-
-    def from_v(b, i):
-        vv = wrap(v - i, side)
-        tile = weight_part(b * zs, zs, core, u, vv, 1)
-        return remote(tile, tile, p1_send.at[b * side + i], p1_recv.at[b * side + i], at_uv(u, vv))
+            tile, tile, p1_send, p1_recv.at[b], at_uv(u, wrap(v + i, side))
+        )
 
     def along_u(b, i):
         part = weight_part(b * zs, zs, core, u, 0, side)
         return remote(
-            part, part, p2_send.at[b * side + i], p2_recv.at[b * side + i], at_uv(wrap(u + i, side), v)
+            part, part, p2_send, p2_recv.at[b * side + i], at_uv(wrap(u + i, side), v)
         )
 
     def from_u(b, i):
         uu = wrap(u - i, side)
         part = weight_part(b * zs, zs, core, uu, 0, side)
-        return remote(part, part, p2_send.at[b * side + i], p2_recv.at[b * side + i], at_uv(uu, v))
+        return remote(part, part, p2_send, p2_recv.at[b * side + i], at_uv(uu, v))
 
     def hand(b, i):
         part = weight_part(b * zs, zs, core, wrap(u - i, side), 0, side)
-        return remote(part, part, sb_send.at[b * side + i], sb_recv.at[b * side + i], sibling)
-
-    def take(b, i):
-        part = weight_part(b * zs, zs, 1 - core, wrap(v - i, side), 0, side)
-        return remote(part, part, sb_send.at[b * side + i], sb_recv.at[b * side + i], sibling)
-
-    def hand_first(b, cc):
-        part = tile_w.at[pl.ds(b * zs, zs), cc]
-        return remote(part, part, fs_send.at[b], fs_recv.at[b], sibling)
+        return remote(part, part, sb_send, sb_recv, sibling)
+
+    def hand_first(b):
+        part = tile_w.at[pl.ds(b * zs, zs), core]
+        return remote(part, part, fs_send, fs_recv, sibling)
 
     def first_block_in(n):
         b = block_at(n)
-        for k in range(zs):
-
-            @pl.when(b * zs + k != z)
-            def _():
-                first_from_z(b * zs + k).wait_recv()
-
-        hand_first(b, core).start()
+        others = zs - 1 if n == 0 else zs
+        if others:
+            arrived(tile_w.at[pl.ds(b * zs, others), core], fz_recv.at[b], sibling)
+        hand_first(b).start()
 
     def hid_block_in(n):
         b = block_at(n)
-        for k in range(zs):
-
-            @pl.when(b * zs + k != z)
-            def _():
-                hid_from_z(b * zs + k).wait_recv()
-
+        others = zs - 1 if n == 0 else zs
+        if others:
+            arrived(weight_part(b * zs, others, core, u, v, 1), az_recv.at[b], sibling)
         for i in range(1, side):
             along_v(b, i).start()
 
     def v_in_block(n):
         b = block_at(n)
-        for i in range(1, side):
-            from_v(b, i).wait_recv()
+        arrived(weight_part(b * zs, zs, core, u, 0, side - 1), p1_recv.at[b], sibling)
         for i in range(1, side):
             along_u(b, i).start()
         hand(b, 0).start()
@@ -258,8 +242,8 @@
     first_block_in(3)
     v_in_block(0)
 
-    each(1, planes, lambda i: feats_from(i).wait_recv())
-    each(0, 4, lambda b: hand_first(b, 1 - core).wait_recv())
+    arrived(plane_feats.at[0:planes - 1], fp_recv, sibling)
+    arrived(tile_w.at[:, 1 - core], fs_recv, sibling)
     part_proj[...] = jnp.dot(
         plane_feats[...].reshape(planes * blk, feat), tile_w[...].reshape(feat, tile_cols),
         preferred_element_type=F32,
@@ -271,11 +255,7 @@
 
     def proj_to(i):
         p = wrap(mine + i, planes)
-        return remote(part_proj.at[p], proj_tile(mine), pp_send.at[i], pp_recv.at[i], {"region": p})
-
-    def proj_from(i):
-        p = wrap(mine - i, planes)
-        return remote(part_proj.at[p], proj_tile(p), pp_send.at[i], pp_recv.at[i], {"region": p})
+        return remote(part_proj.at[p], proj_tile(mine), pp_send, pp_recv, {"region": p})
 
     each(1, planes, lambda i: proj_to(i).start())
     keep_proj = pltpu.make_async_copy(part_proj.at[mine], proj_tile(mine), local_sem.at[3])
@@ -288,11 +268,11 @@
     v_in_block(2)
     u_in_block(0)
     keep_proj.wait()
-    each(1, planes, lambda i: proj_from(i).wait_recv())
+    arrived(part_proj.at[0:planes - 1], pp_recv, sibling)
 
     def halo(by):
         return remote(
-            own_proj.at[1], window.at[2 - by], halo_send.at[by + 2], halo_recv.at[by + 2],
+            own_proj.at[1], window.at[2 - by], halo_send, halo_recv,
             {"shard": wrap(pos + by, shards)},
         )
 
@@ -303,8 +283,7 @@
     u_in_block(1)
     u_in_block(2)
     u_in_block(3)
-    for by in (-2, -1, 1, 2):
-        halo(by).wait_recv()
+    arrived(window.at[0:4], halo_recv, sibling)
 
     rows = 5 * blk
     dest = window[...].reshape(rows, hid)
@@ -315,7 +294,7 @@
     anchor_top = anchor.astype(BF16)
     proj[rows:rows + blk] = anchor_top
     proj[128 + rows:128 + rows + blk] = (anchor - anchor_top.astype(F32)).astype(BF16)
-    each(0, 4 * side, lambda i: take(i // side, i % side).wait_recv())
+    arrived(weights.at[:, 1 - core], sb_recv, sibling)
 
     group = 4
     size = group * slots
@@ -370,19 +349,11 @@
     extra[8:16, :] = jnp.where(row == 0, numer, jnp.where(row == 1, total, 0.0))
 
     def extra_to_z(i):
-        return remote(extra, extra_z.at[z], ez_send.at[i], ez_recv.at[i], at_z(wrap(z + i, depth)))
-
-    def extra_from_z(i):
-        where = wrap(z - i, depth)
-        return remote(extra, extra_z.at[where], ez_send.at[i], ez_recv.at[i], at_z(where))
+        return remote(extra, extra_z.at[z], ez_send, ez_recv, at_z(wrap(z + i, depth)))
 
     def extra_to_plane(i):
         to = {"region": wrap(mine + i, planes)}
-        return remote(extra_zsum, extra_plane.at[mine], ep_send.at[i], ep_recv.at[i], to)
-
-    def extra_from_plane(i):
-        p = wrap(mine - i, planes)
-        return remote(extra_zsum, extra_plane.at[p], ep_send.at[i], ep_recv.at[i], {"region": p})
+        return remote(extra_zsum, extra_plane.at[mine], ep_send, ep_recv, to)
 
     each(1, depth, lambda i: extra_to_z(i).start())
     extra_z[z] = extra[...]
@@ -395,7 +366,7 @@
 
     def to_sibling(n):
         return remote(
-            grad.at[:, 1 - core, :, :, turn(n)], sib_grad.at[:, :, :, turn(n)], gs_send.at[n], gs_recv.at[n], sibling
+            grad.at[:, 1 - core, :, :, turn(n)], sib_grad.at[:, :, :, turn(n)], gs_send, gs_recv.at[n], sibling
         )
 
     def grads(n):
@@ -410,14 +381,7 @@
         inside = pl.ds(pl.multiple_of((n % 2) * wide, wide), wide)
         return remote(
             chip_grad.at[:, h, :, turn(n)], u_in.at[u, :, :, inside],
-            gu_send.at[n * 2 + h], gu_recv.at[u * 2 + n % 2], at_uv(uu, v),
-        )
-
-    def from_u_grad(uu, k):
-        inside = pl.ds(pl.multiple_of(k * wide, wide), wide)
-        return remote(
-            chip_grad.at[:, 0, :, 0:wide], u_in.at[uu, :, :, inside],
-            gu_send.at[0], gu_recv.at[uu * 2 + k], at_uv(uu, v),
+            gu_send, gu_recv, at_uv(uu, v),
         )
 
     def join(n):
@@ -435,16 +399,9 @@
     def to_v(i):
         vv = wrap(v + i, side)
         part = u_sum.at[:, :, pl.ds(pl.multiple_of(vv * tile_cols, tile_cols), tile_cols)]
-        return remote(part, v_in.at[v], gv_send.at[i], gv_recv.at[i], at_uv(u, vv))
-
-    def from_v_grad(i):
-        vv = wrap(v - i, side)
-        part = u_sum.at[:, :, 0:tile_cols]
-        return remote(part, v_in.at[vv], gv_send.at[i], gv_recv.at[i], at_uv(u, vv))
-
-    for i in range(1, side):
-        for k in range(2):
-            from_u_grad(wrap(u + i, side), k).wait_recv()
+        return remote(part, v_in.at[v], gv_send, gv_recv, at_uv(u, vv))
+
+    arrived(u_in.at[0:side - 1], gu_recv, sibling)
 
     own_group = span(u, 0, side)
 
@@ -458,21 +415,16 @@
     for i in range(1, side):
         to_v(i).start()
 
-    each(1, depth, lambda i: extra_from_z(i).wait_recv())
+    arrived(extra_z.at[0:depth - 1], ez_recv, sibling)
     extra_zsum[...] = jnp.sum(extra_z[...], axis=0)
     each(1, planes, lambda i: extra_to_plane(i).start())
     extra_plane[mine] = extra_zsum[...]
 
     def to_z(i):
         where = wrap(z + i, depth)
-        return remote(plane_sum.at[where], z_in.at[z], gz_send.at[i], gz_recv.at[i], at_z(where))
-
-    def from_z(i):
-        where = wrap(z - i, depth)
-        return remote(plane_sum.at[where], z_in.at[where], gz_send.at[i], gz_recv.at[i], at_z(where))
-
-    for i in range(1, side):
-        from_v_grad(i).wait_recv()
+        return remote(plane_sum.at[where], z_in.at[z], gz_send, gz_recv, at_z(where))
+
+    arrived(v_in.at[0:side - 1], gv_recv, sibling)
     own_cols = pl.ds(pl.multiple_of(v * tile_cols, tile_cols), tile_cols)
     acc = u_sum[:, :, own_cols].astype(F32)
     for k in range(1, side):
@@ -481,7 +433,7 @@
     each(1, depth, lambda i: to_z(i).start())
     z_in[z] = plane_sum[z]
 
-    each(1, planes, lambda i: extra_from_plane(i).wait_recv())
+    arrived(extra_plane.at[0:planes - 1], ep_recv, sibling)
     extra_psum[...] = jnp.sum(extra_plane[...], axis=0)
     extra_swap = remote(extra_psum, extra_sib, es_send, es_recv, sibling)
     extra_swap.start()
@@ -491,7 +443,7 @@
     gout_out[...] = sums_all[0:8, :] * inverse
     loss_out[...] = sums_all[8:9, 0:1] * inverse[:, 0:1]
 
-    each(1, depth, lambda i: from_z(i).wait_recv())
+    arrived(z_in.at[0:depth - 1], gz_recv, sibling)
     own_rows[...] = jnp.sum(z_in[...].astype(F32), axis=0) * inverse[0:1, 0:1]
 
     def out_tile(p):
@@ -502,51 +454,31 @@
 
     def share(i):
         to = {"region": wrap(mine + i, planes)}
-        return remote(own_rows, out_tile(mine), ga_send.at[i], ga_recv.at[i], to)
-
-    def shared(i):
-        p = wrap(mine - i, planes)
-        return remote(own_rows, out_tile(p), ga_send.at[i], ga_recv.at[i], {"region": p})
+        return remote(own_rows, out_tile(mine), ga_send, ga_recv, to)
 
     each(1, planes, lambda i: share(i).start())
     own_out = pltpu.make_async_copy(own_rows, out_tile(mine), local_sem.at[1])
     own_out.start()
 
-    for by in (-2, -1, 1, 2):
-        halo(by).wait_send()
-    each(1, depth, lambda i: first_to_z(i, anchor_hbm).wait_send())
-    each(1, depth, lambda i: hid_to_z(i).wait_send())
-    each(0, 4, lambda b: hand_first(b, core).wait_send())
-    each(1, planes, lambda i: feats_to(i).wait_send())
-    each(1, planes, lambda i: proj_to(i).wait_send())
-
-    def weights_left(b):
-        for i in range(1, side):
-            along_v(b, i).wait_send()
-            along_u(b, i).wait_send()
-        for i in range(side):
-            hand(b, i).wait_send()
-
-    each(0, 4, weights_left)
-    each(1, depth, lambda i: extra_to_z(i).wait_send())
-    each(1, planes, lambda i: extra_to_plane(i).wait_send())
+    left(tile_w.at[0:depth - 1, core], fz_send, sibling)
+    left(tile_w.at[0:depth - 1, core], az_send, sibling)
+    left(tile_w.at[:, core], fs_send, sibling)
+    left(plane_feats.at[0:planes - 1], fp_send, sibling)
+    left(part_proj.at[0:planes - 1], pp_send, sibling)
+    left(window.at[0:4], halo_send, sibling)
+    left(weight_part(0, depth, core, u, 0, side - 1), p1_send, sibling)
+    left(weights.at[0:(side - 1) * depth // side, core], p2_send, sibling)
+    left(weights.at[:, core], sb_send, sibling)
+    left(sib_grad, gs_send, sibling)
+    left(u_in.at[0:side - 1], gu_send, sibling)
+    left(v_in.at[0:side - 1], gv_send, sibling)
+    left(z_in.at[0:depth - 1], gz_send, sibling)
+    left(extra_z.at[0:depth - 1], ez_send, sibling)
+    left(extra_plane.at[0:planes - 1], ep_send, sibling)
     extra_swap.wait_send()
-    each(0, turns, lambda n: to_sibling(n).wait_send())
-
-    def u_left(n):
-        for h in range(2):
-
-            @pl.when(h * per_half + n // 2 != u)
-            def _():
-                to_u(n, h).wait_send()
-
-    each(0, turns, u_left)
-    for i in range(1, side):
-        to_v(i).wait_send()
-    each(1, depth, lambda i: to_z(i).wait_send())
     own_out.wait()
-    each(1, planes, lambda i: shared(i).wait_recv())
-    each(1, planes, lambda i: share(i).wait_send())
+    arrived(part_proj.at[0:planes - 1], ga_recv, sibling)
+    left(part_proj.at[0:planes - 1], ga_send, sibling)
 
 
 def shards(tiles, tile_block, neighbors, counts, flows, w_anchor, w_dest, w_hidden, w_out):
@@ -563,6 +495,7 @@
     vmem = pl.BlockSpec(memory_space=pltpu.VMEM)
     hbm = pl.BlockSpec(memory_space=pltpu.HBM)
     dma = lambda n: pltpu.SemaphoreType.DMA((n,))
+    one = pltpu.SemaphoreType.DMA
     scratch = [
         pltpu.VMEM(tiles.shape, BF16),
         pltpu.VMEM((1, tile_block.shape[0]), jnp.int32),
@@ -597,11 +530,10 @@
         pltpu.VMEM((planes, 16, width), F32),
         pltpu.VMEM((16, width), F32),
         pltpu.VMEM((16, width), F32),
-        dma(5), dma(5), dma(depth), dma(depth), dma(4), dma(4), dma(planes), dma(planes), dma(planes), dma(planes),
-        dma(depth), dma(depth), dma(4 * side), dma(4 * side), dma(4 * side), dma(4 * side),
-        dma(4 * side), dma(4 * side), dma(turns), dma(turns), dma(2 * turns), dma(2 * side), dma(side), dma(side),
-        dma(depth), dma(depth), dma(planes), dma(planes), dma(depth), dma(depth), dma(planes), dma(planes),
-        pltpu.SemaphoreType.DMA, pltpu.SemaphoreType.DMA, dma(6), dma(4),
+        one, one, one, dma(4), one, one, one, one, one, one,
+        one, dma(4), one, dma(4), one, dma(4 * side), one, one,
+        one, dma(turns), one, one, one, one, one, one,
+        one, one, one, one, one, one, one, one, dma(6), dma(4),
     ]
     grad, gout, loss = pl.pallas_call(
         functools.partial(step_kernel, (side, depth, blk, slots, hid)),
@@ -611,7 +543,7 @@
             jax.ShapeDtypeStruct((1, 1), F32),
         ),
         in_specs=[hbm] * 9,
-        out_specs=(vmem, vmem, vmem),
+        out_specs=(hbm, vmem, vmem),
         scratch_shapes=scratch,
         compiler_params=pltpu.CompilerParams(
             collective_id=0, has_side_effects=True, vmem_limit_bytes=62 * 2 ** 20

time: 86.2 us -> 82.9 us (0.962)
  the two profiles are of different devices: /device:TPU:1 before, /device:TPU:4 now
where the time goes in v4:
time: 82.9 us; the launch traced here: 82.6 us
  Pallas kernels  78.1 us (94%)
  between operations  2.41 us (3%)
  local copies, waits for them, and re-layouts  2.17 us (3%)
    pallas_call x1, Pallas kernels, shards(): pl.pallas_call(functools.partial(step_kernel, (side, depth, blk, slots, h...  78.1 us
    unnamed x4, local copies, waits for them, and re-layouts  2.17 us

profile of v4, /device:TPU:4, one launch (start us, length us, event | category | flops | bytes accessed | tf_op | source)
XLA Modules:
  0.0 82.6 jit_solution(15916980966681471351)
XLA Ops:
  0.6 78.1 %shard_map.112 = (f32[32,1024]{1,0:T(8,128)}, f32[8,128]{1,0:T(8,128)}, f32[1,1]{1,0:T(1,128)}) custom-call(bf16[1024,512]{1,0:T(8,128)(2,1)} %tiles_hbm.1, s32[1,1024]{1,0:T(1,128)} %bitcast.4, s32[16,64]{1,0:T(8,128)} %neighbors_hbm.1, s32[16]{0:T(128)} %counts_hbm.1, s32[16,64]{1,0:T(8,128)} %flows_hbm.1, bf16[16,1024]{1,0:T(8,128)(2,1)} %anchor_hbm.1, ...), custom_call_target="tpu_custom_call" | custom-call | flops 4294967296 | bytes 1048576 | tf_op jit(solution)/shard_map/pallas_call | solution.py:538
  78.7 0.0 copy-start
  78.7 1.6 %copy.15 = f32[32,1024]{1,0:T(8,128)} copy(f32[32,1024]{1,0:T(8,128)} %get-tuple-element.12) | data formatting | bytes 262144
  80.3 0.0 copy-done
  80.3 0.6 copy.16
Async XLA Ops:
  78.7 1.6 %copy-start = (f32[8,128]{1,0:T(8,128)S(1)}, f32[8,128]{1,0:T(8,128)}, u32[]{:S(2)}) copy-start(f32[8,128]{1,0:T(8,128)} %get-tuple-element.7) | copy-start | bytes 12292

commit v5 on v4

--- a/solution.py
+++ b/solution.py
@@ -31,7 +31,7 @@
     tiles_hbm, tile_block_hbm, neighbors_hbm, counts_hbm, flows_hbm, anchor_hbm, dest_hbm, hidden_hbm, out_hbm,
     grad_out, gout_out, loss_out,
     tiles, tile_block, neighbors, counts, flows, w_out,
-    weights, features, tile_w, plane_feats, part_proj, own_proj, window, proj, onehot, first_t, active, pre, grad, sib_grad, chip_grad, u_in, u_sum, v_in,
+    weights, features, tile_w, plane_feats, part_proj, own_proj, window, proj, onehot, first, first_t, lanes, out_weight, active, pre, grad, sib_grad, chip_grad, u_in, u_sum, v_in,
     plane_sum, z_in, own_rows, extra, extra_z, extra_zsum, extra_plane, extra_psum, extra_sib,
     halo_send, halo_recv, fz_send, fz_recv, fs_send, fs_recv, fp_send, fp_recv, pp_send, pp_recv,
     az_send, az_recv, p1_send, p1_recv, p2_send, p2_recv, sb_send, sb_recv,
@@ -238,9 +238,10 @@
     first_block_in(0)
     hid_block_in(0)
     first_block_in(1)
+    v_in_block(0)
     first_block_in(2)
     first_block_in(3)
-    v_in_block(0)
+    hid_block_in(1)
 
     arrived(plane_feats.at[0:planes - 1], fp_recv, sibling)
     arrived(tile_w.at[:, 1 - core], fs_recv, sibling)
@@ -261,7 +262,6 @@
     keep_proj = pltpu.make_async_copy(part_proj.at[mine], proj_tile(mine), local_sem.at[3])
     keep_proj.start()
 
-    hid_block_in(1)
     hid_block_in(2)
     v_in_block(1)
     hid_block_in(3)
@@ -294,28 +294,41 @@
     anchor_top = anchor.astype(BF16)
     proj[rows:rows + blk] = anchor_top
     proj[128 + rows:128 + rows + blk] = (anchor - anchor_top.astype(F32)).astype(BF16)
-    arrived(weights.at[:, 1 - core], sb_recv, sibling)
 
     group = 4
     size = group * slots
-    weight = w_out[...].astype(F32).reshape(1, hid)
-
-    def score(i, scores):
-        at = pl.multiple_of(i * size, size)
-        pick = onehot[pl.ds(at, size), :]
-        both = jnp.concatenate([pick, pick], axis=1)
-        first = jnp.maximum(jnp.dot(both, proj[...], preferred_element_type=F32), 0.0).astype(BF16)
-        first_t[:, pl.ds(at, size)] = first.T
+    wide = group_cols // 2
+    turns = hid // wide
+
+    def turn(n):
+        return pl.ds(pl.multiple_of(n * wide, wide), wide)
+
+    def hidden(n):
+        both = jnp.concatenate([onehot[...], onehot[...]], axis=1)
+        part = jnp.maximum(jnp.dot(both, proj[:, turn(n)], preferred_element_type=F32), 0.0).astype(BF16)
+        first[:, turn(n)] = part
+        first_t[turn(n), :] = part.T
+
+    each(0, turns, hidden)
+    arrived(weights.at[:, 1 - core], sb_recv, sibling)
+
+    out_weight[...] = w_out[...].astype(F32).reshape(1, hid)
+
+    def score(n):
         act = jnp.maximum(
-            jnp.dot(first, weights[...].reshape(hid, hid), preferred_element_type=F32), 0.0
-        )
-        active[pl.ds(at, size), :] = act
-        col = jnp.sum(act * weight, axis=1, keepdims=True)
-        for a in range(group):
-            scores = jnp.where(lane16 == i * group + a, col[a * slots:(a + 1) * slots], scores)
-        return scores
-
-    scores = lax.fori_loop(0, blk // group, score, jnp.zeros((slots, blk), F32))
+            jnp.dot(first[...], weights[:, :, :, :, turn(n)].reshape(hid, wide), preferred_element_type=F32), 0.0
+        )
+        active[:, turn(n)] = act
+        part = act * out_weight[:, turn(n)]
+        lanes[...] += sum(part[:, k:k + 128] for k in range(0, wide, 128))
+
+    lanes[...] = jnp.zeros_like(lanes)
+    each(0, turns, score)
+    col = jnp.sum(lanes[...], axis=1, keepdims=True)
+    scores = jnp.zeros((slots, blk), F32)
+    for b in range(blk):
+        scores = jnp.where(lane16 == b, col[b * slots:(b + 1) * slots], scores)
+    weight = out_weight[...]
 
     top = jnp.max(jnp.where(valid, scores, -jnp.inf), axis=0, keepdims=True)
     expo = jnp.where(valid, jnp.exp(scores - top), 0.0)
@@ -326,43 +339,20 @@
     numer = -jnp.sum(jnp.where(valid, flow * logp, 0.0))
     total = jnp.sum(anchor_total)
 
-    def back(i, gout):
-        at = pl.multiple_of(i * size, size)
-        col = jnp.concatenate(
+    def pair_grads(i):
+        return jnp.concatenate(
             [
                 jnp.sum(jnp.where(lane16 == i * group + a, sgrad, 0.0), axis=1, keepdims=True)
                 for a in range(group)
             ],
             axis=0,
         )
-        act = active[pl.ds(at, size), :]
-        pre[pl.ds(at, size), :] = jnp.where(act > 0, col * weight, 0.0).astype(BF16)
-        return gout + jnp.sum((col * act).reshape(size // 8, 8, hid), axis=0)
-
-    gout = lax.fori_loop(0, blk // group, back, jnp.zeros((8, hid), F32))
-    gout = jnp.sum(gout, axis=0, keepdims=True)
-
-    width = hid // 8
-    for r in range(8):
-        extra[r:r + 1, :] = gout[:, r * width:(r + 1) * width]
-    row = lax.broadcasted_iota(jnp.int32, (8, width), 0)
-    extra[8:16, :] = jnp.where(row == 0, numer, jnp.where(row == 1, total, 0.0))
-
-    def extra_to_z(i):
-        return remote(extra, extra_z.at[z], ez_send, ez_recv, at_z(wrap(z + i, depth)))
-
-    def extra_to_plane(i):
-        to = {"region": wrap(mine + i, planes)}
-        return remote(extra_zsum, extra_plane.at[mine], ep_send, ep_recv, to)
-
-    each(1, depth, lambda i: extra_to_z(i).start())
-    extra_z[z] = extra[...]
-
-    wide = group_cols // 2
-    turns = hid // wide
-
-    def turn(n):
-        return pl.ds(pl.multiple_of(n * wide, wide), wide)
+
+    def back(i):
+        at = pl.multiple_of(i * size, size)
+        pre[pl.ds(at, size), :] = jnp.where(active[pl.ds(at, size), :] > 0, pair_grads(i) * weight, 0.0).astype(BF16)
+
+    each(0, blk // group, back)
 
     def to_sibling(n):
         return remote(
@@ -373,8 +363,6 @@
         part = jnp.dot(first_t[...], pre[:, turn(n)], preferred_element_type=F32)
         grad[:, :, :, :, turn(n)] = part.reshape(depth, 2, 2, 16, wide).astype(BF16)
         to_sibling(n).start()
-
-    each(0, turns, grads)
 
     def to_u(n, h):
         uu = h * per_half + n // 2
@@ -394,7 +382,35 @@
             def _():
                 to_u(n, h).start()
 
-    each(0, turns, join)
+    behind = 2
+
+    def step(n):
+        pl.when(n < turns)(lambda: grads(n))
+        pl.when(n >= behind)(lambda: join(n - behind))
+
+    each(0, turns + behind, step)
+
+    def output_grad(i, acc):
+        at = pl.multiple_of(i * size, size)
+        return acc + jnp.sum((pair_grads(i) * active[pl.ds(at, size), :]).reshape(size // 8, 8, hid), axis=0)
+
+    gout = lax.fori_loop(0, blk // group, output_grad, jnp.zeros((8, hid), F32))
+    gout = jnp.sum(gout, axis=0, keepdims=True)
+    width = hid // 8
+    for r in range(8):
+        extra[r:r + 1, :] = gout[:, r * width:(r + 1) * width]
+    row = lax.broadcasted_iota(jnp.int32, (8, width), 0)
+    extra[8:16, :] = jnp.where(row == 0, numer, jnp.where(row == 1, total, 0.0))
+
+    def extra_to_z(i):
+        return remote(extra, extra_z.at[z], ez_send, ez_recv, at_z(wrap(z + i, depth)))
+
+    def extra_to_plane(i):
+        to = {"region": wrap(mine + i, planes)}
+        return remote(extra_zsum, extra_plane.at[mine], ep_send, ep_recv, to)
+
+    each(1, depth, lambda i: extra_to_z(i).start())
+    extra_z[z] = extra[...]
 
     def to_v(i):
         vv = wrap(v + i, side)
@@ -414,11 +430,6 @@
     each(0, 4, sum_u)
     for i in range(1, side):
         to_v(i).start()
-
-    arrived(extra_z.at[0:depth - 1], ez_recv, sibling)
-    extra_zsum[...] = jnp.sum(extra_z[...], axis=0)
-    each(1, planes, lambda i: extra_to_plane(i).start())
-    extra_plane[mine] = extra_zsum[...]
 
     def to_z(i):
         where = wrap(z + i, depth)
@@ -430,8 +441,19 @@
     for k in range(1, side):
         acc = acc + v_in[wrap(v + k, side)].astype(F32)
     plane_sum[...] = acc.astype(BF16)
-    each(1, depth, lambda i: to_z(i).start())
+    to_z(depth // 2).start()
+
+    def to_both(i):
+        to_z(depth // 2 + i).start()
+        to_z(depth // 2 - i).start()
+
+    each(1, depth // 2, to_both)
     z_in[z] = plane_sum[z]
+
+    arrived(extra_z.at[0:depth - 1], ez_recv, sibling)
+    extra_zsum[...] = jnp.sum(extra_z[...], axis=0)
+    each(1, planes, lambda i: extra_to_plane(i).start())
+    extra_plane[mine] = extra_zsum[...]
 
     arrived(extra_plane.at[0:planes - 1], ep_recv, sibling)
     extra_psum[...] = jnp.sum(extra_plane[...], axis=0)
@@ -452,11 +474,10 @@
         vv = px + core * (py - px)
         return grad_out.at[pl.ds(pl.multiple_of((uu // per_half) * 16, 16), 16), span(uu, vv, 1)]
 
-    def share(i):
-        to = {"region": wrap(mine + i, planes)}
-        return remote(own_rows, out_tile(mine), ga_send, ga_recv, to)
-
-    each(1, planes, lambda i: share(i).start())
+    far_first = sorted(range(1, planes), key=lambda i: -sum(min(d, side - d) for d in divmod(i, side)))
+    for i in far_first:
+        to = at_uv(wrap(u + i // side, side), wrap(v + i % side, side))
+        remote(own_rows, out_tile(mine), ga_send, ga_recv, to).start()
     own_out = pltpu.make_async_copy(own_rows, out_tile(mine), local_sem.at[1])
     own_out.start()
 
@@ -512,7 +533,10 @@
         pltpu.VMEM((5, blk, hid), F32),
         pltpu.VMEM((256, hid), BF16),
         pltpu.VMEM((pairs, 128), BF16),
+        pltpu.VMEM((pairs, hid), BF16),
         pltpu.VMEM((hid, pairs), BF16),
+        pltpu.VMEM((pairs, 128), F32),
+        pltpu.VMEM((1, hid), F32),
         pltpu.VMEM((pairs, hid), F32),
         pltpu.VMEM((pairs, hid), BF16),
         pltpu.VMEM((depth, 2, 2, 16, hid), BF16),

time: 82.9 us -> 81.2 us (0.979)
  the two profiles are of different devices: /device:TPU:4 before, /device:TPU:2 now
where the time goes in v5:
time: 81.2 us; the launch traced here: 81 us
  Pallas kernels  76.4 us (94%)
  between operations  2.41 us (3%)
  local copies, waits for them, and re-layouts  2.17 us (3%)
    pallas_call x1, Pallas kernels, shards(): pl.pallas_call(functools.partial(step_kernel, (side, depth, blk, slots, h...  76.4 us
    unnamed x4, local copies, waits for them, and re-layouts  2.17 us

profile of v5, /device:TPU:2, one launch (start us, length us, event | category | flops | bytes accessed | tf_op | source)
XLA Modules:
  0.0 81.0 jit_solution(17127931808561018312)
XLA Ops:
  0.6 76.4 %shard_map.112 = (f32[32,1024]{1,0:T(8,128)}, f32[8,128]{1,0:T(8,128)}, f32[1,1]{1,0:T(1,128)}) custom-call(bf16[1024,512]{1,0:T(8,128)(2,1)} %tiles_hbm.1, s32[1,1024]{1,0:T(1,128)} %bitcast.4, s32[16,64]{1,0:T(8,128)} %neighbors_hbm.1, s32[16]{0:T(128)} %counts_hbm.1, s32[16,64]{1,0:T(8,128)} %flows_hbm.1, bf16[16,1024]{1,0:T(8,128)(2,1)} %anchor_hbm.1, ...), custom_call_target="tpu_custom_call" | custom-call | flops 4294967296 | bytes 1048576 | tf_op jit(solution)/shard_map/pallas_call | solution.py:562
  77.0 0.0 copy-start
  77.0 1.6 %copy.15 = f32[32,1024]{1,0:T(8,128)} copy(f32[32,1024]{1,0:T(8,128)} %get-tuple-element.12) | data formatting | bytes 262144
  78.6 0.0 copy-done
  78.6 0.6 copy.16
Async XLA Ops:
  77.0 1.6 %copy-start = (f32[8,128]{1,0:T(8,128)S(1)}, f32[8,128]{1,0:T(8,128)}, u32[]{:S(2)}) copy-start(f32[8,128]{1,0:T(8,128)} %get-tuple-element.7) | copy-start | bytes 12292

commit v6 on v5

--- a/solution.py
+++ b/solution.py
@@ -33,8 +33,8 @@
     tiles, tile_block, neighbors, counts, flows, w_out,
     weights, features, tile_w, plane_feats, part_proj, own_proj, window, proj, onehot, first, first_t, lanes, out_weight, active, pre, grad, sib_grad, chip_grad, u_in, u_sum, v_in,
     plane_sum, z_in, own_rows, extra, extra_z, extra_zsum, extra_plane, extra_psum, extra_sib,
-    halo_send, halo_recv, fz_send, fz_recv, fs_send, fs_recv, fp_send, fp_recv, pp_send, pp_recv,
-    az_send, az_recv, p1_send, p1_recv, p2_send, p2_recv, sb_send, sb_recv,
+    halo_send, halo_recv, fz_send, fz_recv, fz_pass, fs_send, fs_recv, fp_send, fp_recv, pp_send, pp_recv,
+    az_send, az_recv, az_pass, p1_send, p1_recv, p2_send, p2_recv, sb_send, sb_recv,
     gs_send, gs_recv, gu_send, gu_recv, gv_send, gv_recv, gz_send, gz_recv,
     ga_send, ga_recv, ez_send, ez_recv, ep_send, ep_recv, es_send, es_recv, load_sem, local_sem,
 ):
@@ -84,12 +84,14 @@
     def greet(where):
         pl.semaphore_signal(barrier, inc=1, device_id=where, device_id_type=MESH)
 
+    zs = depth // 4
+    first_block = z // zs
+
     def greet_z(i):
-        greet(at_z(wrap(z + depth // 2 + i, depth)))
-        greet(at_z(wrap(z + depth // 2 - i, depth)))
-
-    greet(at_z(wrap(z + depth // 2, depth)))
-    each(1, depth // 2, greet_z)
+        greet(at_z(wrap(z + zs - i, depth)))
+        greet(at_z(wrap(z + i - zs, depth)))
+
+    each(0, zs, greet_z)
     each(1, planes, lambda i: greet({"region": wrap(mine + i, planes)}))
     greet(cross)
     greet(sibling)
@@ -111,37 +113,47 @@
     def weight_slot(where):
         return weights.at[where, core, u // per_half, :, span(u, v, 1)]
 
-    zs = depth // 4
-    first_block = z // zs
-
-    def first_to_z(i, source):
-        to = at_z(wrap(z + i, depth))
-        return remote(source.at[:, first_cols], tile_w.at[z, core], fz_send, fz_recv.at[first_block], to)
-
-    def hid_to_z(i):
-        to = at_z(wrap(z + i, depth))
-        return remote(hid_tile, weight_slot(z), az_send, az_recv.at[first_block], to)
+    def first_to_z(by, source, far=None):
+        sem = fz_recv.at[first_block] if far is None else fz_pass.at[far]
+        return remote(source.at[:, first_cols], tile_w.at[z, core], fz_send, sem, at_z(wrap(z + by, depth)))
+
+    def hid_to_z(by, far=None):
+        sem = az_recv.at[first_block] if far is None else az_pass.at[far]
+        return remote(hid_tile, weight_slot(z), az_send, sem, at_z(wrap(z + by, depth)))
 
     def keep_first(source):
         return pltpu.make_async_copy(source.at[:, first_cols], tile_w.at[z, core], local_sem.at[2])
 
-    def near_first(start):
+    def spread_z(copy_to):
+        copy_to(zs, 0).start()
+        copy_to(-zs, 1).start()
+
         def both_ways(i):
-            start(i)
-            start(depth - i)
-
-        each(1, depth // 2, both_ways)
-        start(depth // 2)
-
-    pl.semaphore_wait(barrier, planes - 1 + depth - 1 + 2)
+            copy_to(zs - i).start()
+            copy_to(i - zs).start()
+
+        each(1, zs, both_ways)
+
+    def pass_on(slot_of, send, recv, passed):
+        for far, sign in ((0, 1), (1, -1)):
+            slot = slot_of(wrap(z - sign * zs, depth))
+            arrived(slot, passed.at[far], sibling)
+            sem = recv.at[wrap(first_block - sign, 4)]
+
+            def onward(i):
+                remote(slot, slot, send, sem, at_z(wrap(z + sign * (zs - i), depth))).start()
+
+            each(far, zs, onward)
+
+    pl.semaphore_wait(barrier, planes - 1 + 2 * zs + 2)
     for k, source in enumerate((anchor_hbm, dest_hbm)):
 
         @pl.when(matrix == k)
         def _():
-            near_first(lambda i: first_to_z(i, source).start())
+            spread_z(lambda by, far=None: first_to_z(by, source, far))
             keep_first(source).start()
 
-    near_first(lambda i: hid_to_z(i).start())
+    spread_z(hid_to_z)
     keep_tile = pltpu.make_async_copy(hid_tile, weight_slot(z), local_sem.at[0])
     keep_tile.start()
 
@@ -158,6 +170,8 @@
         return remote(features, plane_feats.at[mine], fp_send, fp_recv, {"region": p})
 
     each(1, planes, lambda i: feats_to(i).start())
+    pass_on(lambda where: tile_w.at[where, core], fz_send, fz_recv, fz_pass)
+    pass_on(weight_slot, az_send, az_recv, az_pass)
 
     shift = mine * (blk * shards) + (pos - 2) * blk
     for copy in loads[2:]:
@@ -209,14 +223,14 @@
 
     def first_block_in(n):
         b = block_at(n)
-        others = zs - 1 if n == 0 else zs
+        others = zs if n == 3 else zs - 1
         if others:
             arrived(tile_w.at[pl.ds(b * zs, others), core], fz_recv.at[b], sibling)
         hand_first(b).start()
 
     def hid_block_in(n):
         b = block_at(n)
-        others = zs - 1 if n == 0 else zs
+        others = zs if n == 3 else zs - 1
         if others:
             arrived(weight_part(b * zs, others, core, u, v, 1), az_recv.at[b], sibling)
         for i in range(1, side):
@@ -554,8 +568,8 @@
         pltpu.VMEM((planes, 16, width), F32),
         pltpu.VMEM((16, width), F32),
         pltpu.VMEM((16, width), F32),
-        one, one, one, dma(4), one, one, one, one, one, one,
-        one, dma(4), one, dma(4), one, dma(4 * side), one, one,
+        one, one, one, dma(4), dma(2), one, one, one, one, one, one,
+        one, dma(4), dma(2), one, dma(4), one, dma(4 * side), one, one,
         one, dma(turns), one, one, one, one, one, one,
         one, one, one, one, one, one, one, one, dma(6), dma(4),
     ]

time: 81.2 us -> 77.5 us (0.954)
  the two profiles are of different devices: /device:TPU:2 before, /device:TPU:1 now
where the time goes in v6:
time: 77.5 us; the launch traced here: 77.4 us
  Pallas kernels  72.8 us (94%)
  between operations  2.41 us (3%)
  local copies, waits for them, and re-layouts  2.17 us (3%)
    pallas_call x1, Pallas kernels, shards(): pl.pallas_call(functools.partial(step_kernel, (side, depth, blk, slots, h...  72.8 us
    unnamed x4, local copies, waits for them, and re-layouts  2.17 us

profile of v6, /device:TPU:1, one launch (start us, length us, event | category | flops | bytes accessed | tf_op | source)
XLA Modules:
  0.0 77.4 jit_solution(4375069533433631839)
XLA Ops:
  0.6 72.8 %shard_map.112 = (f32[32,1024]{1,0:T(8,128)}, f32[8,128]{1,0:T(8,128)}, f32[1,1]{1,0:T(1,128)}) custom-call(bf16[1024,512]{1,0:T(8,128)(2,1)} %tiles_hbm.1, s32[1,1024]{1,0:T(1,128)} %bitcast.4, s32[16,64]{1,0:T(8,128)} %neighbors_hbm.1, s32[16]{0:T(128)} %counts_hbm.1, s32[16,64]{1,0:T(8,128)} %flows_hbm.1, bf16[16,1024]{1,0:T(8,128)(2,1)} %anchor_hbm.1, ...), custom_call_target="tpu_custom_call" | custom-call | flops 4294967296 | bytes 1048576 | tf_op jit(solution)/shard_map/pallas_call | solution.py:576
  73.4 0.0 copy-start
  73.4 1.6 %copy.15 = f32[32,1024]{1,0:T(8,128)} copy(f32[32,1024]{1,0:T(8,128)} %get-tuple-element.12) | data formatting | bytes 262144
  75.0 0.0 copy-done
  75.0 0.6 copy.16
Async XLA Ops:
  73.4 1.6 %copy-start = (f32[8,128]{1,0:T(8,128)S(1)}, f32[8,128]{1,0:T(8,128)}, u32[]{:S(2)}) copy-start(f32[8,128]{1,0:T(8,128)} %get-tuple-element.7) | copy-start | bytes 12292

commit v7 on v6

--- a/solution.py
+++ b/solution.py
@@ -32,11 +32,11 @@
     grad_out, gout_out, loss_out,
     tiles, tile_block, neighbors, counts, flows, w_out,
     weights, features, tile_w, plane_feats, part_proj, own_proj, window, proj, onehot, first, first_t, lanes, out_weight, active, pre, grad, sib_grad, chip_grad, u_in, u_sum, v_in,
-    plane_sum, z_in, own_rows, extra, extra_z, extra_zsum, extra_plane, extra_psum, extra_sib,
+    plane_sum, z_in, own_rows, extra, extra_sib, extra_own, extra_z, extra_zsum, extra_plane, extra_all,
     halo_send, halo_recv, fz_send, fz_recv, fz_pass, fs_send, fs_recv, fp_send, fp_recv, pp_send, pp_recv,
     az_send, az_recv, az_pass, p1_send, p1_recv, p2_send, p2_recv, sb_send, sb_recv,
     gs_send, gs_recv, gu_send, gu_recv, gv_send, gv_recv, gz_send, gz_recv,
-    ga_send, ga_recv, ez_send, ez_recv, ep_send, ep_recv, es_send, es_recv, load_sem, local_sem,
+    ga_send, ga_recv, ez_send, ez_recv, ep_send, ep_recv, ea_send, ea_recv, es_send, es_recv, load_sem, local_sem,
 ):
     side, depth, blk, slots, hid = dims
     planes = side * side
@@ -256,6 +256,7 @@
     first_block_in(2)
     first_block_in(3)
     hid_block_in(1)
+    hid_block_in(2)
 
     arrived(plane_feats.at[0:planes - 1], fp_recv, sibling)
     arrived(tile_w.at[:, 1 - core], fs_recv, sibling)
@@ -276,9 +277,8 @@
     keep_proj = pltpu.make_async_copy(part_proj.at[mine], proj_tile(mine), local_sem.at[3])
     keep_proj.start()
 
-    hid_block_in(2)
+    hid_block_in(3)
     v_in_block(1)
-    hid_block_in(3)
     v_in_block(2)
     u_in_block(0)
     keep_proj.wait()
@@ -412,56 +412,67 @@
     gout = jnp.sum(gout, axis=0, keepdims=True)
     width = hid // 8
     for r in range(8):
-        extra[r:r + 1, :] = gout[:, r * width:(r + 1) * width]
+        extra[0, r:r + 1, :] = gout[:, r * width:(r + 1) * width]
     row = lax.broadcasted_iota(jnp.int32, (8, width), 0)
-    extra[8:16, :] = jnp.where(row == 0, numer, jnp.where(row == 1, total, 0.0))
+    extra[1] = jnp.where(row == 0, numer, jnp.where(row == 1, total, 0.0))
 
     def extra_to_z(i):
-        return remote(extra, extra_z.at[z], ez_send, ez_recv, at_z(wrap(z + i, depth)))
+        return remote(extra_own, extra_z.at[z], ez_send, ez_recv, at_z(wrap(z + i, depth)))
 
     def extra_to_plane(i):
         to = {"region": wrap(mine + i, planes)}
         return remote(extra_zsum, extra_plane.at[mine], ep_send, ep_recv, to)
 
+    extra_half = remote(extra.at[1 - core], extra_sib, ea_send, ea_recv, sibling)
+    extra_half.start()
+    extra_half.wait_recv()
+    extra_own[...] = extra[core] + extra_sib[...]
     each(1, depth, lambda i: extra_to_z(i).start())
-    extra_z[z] = extra[...]
-
-    def to_v(i):
+    extra_z[z] = extra_own[...]
+
+    def to_v(b, i):
         vv = wrap(v + i, side)
-        part = u_sum.at[:, :, pl.ds(pl.multiple_of(vv * tile_cols, tile_cols), tile_cols)]
-        return remote(part, v_in.at[v], gv_send, gv_recv, at_uv(u, vv))
+        zz = pl.ds(b * zs, zs)
+        part = u_sum.at[zz, :, pl.ds(pl.multiple_of(vv * tile_cols, tile_cols), tile_cols)]
+        return remote(part, v_in.at[v, zz], gv_send, gv_recv.at[b], at_uv(u, vv))
 
     arrived(u_in.at[0:side - 1], gu_recv, sibling)
 
     own_group = span(u, 0, side)
 
+    def far_block(i):
+        return wrap(first_block + 2 - i + (i // 2) * 3 - (i // 3) * 2, 4)
+
     def sum_u(i):
-        acc = chip_grad[pl.ds(i * zs, zs), u // per_half, :, own_group].astype(F32)
+        b = far_block(i)
+        part = pl.ds(b * zs, zs)
+        acc = chip_grad[part, u // per_half, :, own_group].astype(F32)
         for k in range(1, side):
-            acc = acc + u_in[wrap(u + k, side), pl.ds(i * zs, zs)].astype(F32)
-        u_sum[pl.ds(i * zs, zs)] = acc.astype(BF16)
+            acc = acc + u_in[wrap(u + k, side), part].astype(F32)
+        u_sum[part] = acc.astype(BF16)
+        for k in range(1, side):
+            to_v(b, k).start()
 
     each(0, 4, sum_u)
-    for i in range(1, side):
-        to_v(i).start()
-
-    def to_z(i):
-        where = wrap(z + i, depth)
-        return remote(plane_sum.at[where], z_in.at[z], gz_send, gz_recv, at_z(where))
-
-    arrived(v_in.at[0:side - 1], gv_recv, sibling)
+
     own_cols = pl.ds(pl.multiple_of(v * tile_cols, tile_cols), tile_cols)
-    acc = u_sum[:, :, own_cols].astype(F32)
-    for k in range(1, side):
-        acc = acc + v_in[wrap(v + k, side)].astype(F32)
-    plane_sum[...] = acc.astype(BF16)
-    to_z(depth // 2).start()
-
-    def to_both(i):
-        to_z(depth // 2 + i).start()
-        to_z(depth // 2 - i).start()
-
-    each(1, depth // 2, to_both)
+
+    def sum_v(i):
+        b = far_block(i)
+        part = pl.ds(b * zs, zs)
+        arrived(v_in.at[0:side - 1, part], gv_recv.at[b], sibling)
+        acc = u_sum[part, :, own_cols].astype(F32)
+        for k in range(1, side):
+            acc = acc + v_in[wrap(v + k, side), part].astype(F32)
+        plane_sum[part] = acc.astype(BF16)
+        for k in range(zs):
+            where = b * zs + k
+
+            @pl.when(where != z)
+            def _():
+                remote(plane_sum.at[where], z_in.at[z], gz_send, gz_recv, at_z(where)).start()
+
+    each(0, 4, sum_v)
     z_in[z] = plane_sum[z]
 
     arrived(extra_z.at[0:depth - 1], ez_recv, sibling)
@@ -470,14 +481,13 @@
     extra_plane[mine] = extra_zsum[...]
 
     arrived(extra_plane.at[0:planes - 1], ep_recv, sibling)
-    extra_psum[...] = jnp.sum(extra_plane[...], axis=0)
-    extra_swap = remote(extra_psum, extra_sib, es_send, es_recv, sibling)
+    extra_all[core] = jnp.sum(extra_plane[...], axis=0)
+    extra_swap = remote(extra_all.at[core], extra_all.at[core], es_send, es_recv, sibling)
     extra_swap.start()
     extra_swap.wait_recv()
-    sums_all = extra_psum[...] + extra_sib[...]
-    inverse = 1.0 / sums_all[9:10, :]
-    gout_out[...] = sums_all[0:8, :] * inverse
-    loss_out[...] = sums_all[8:9, 0:1] * inverse[:, 0:1]
+    inverse = 1.0 / extra_all[1, 1:2, :]
+    gout_out[...] = extra_all[0] * inverse
+    loss_out[...] = extra_all[1, 0:1, 0:1] * inverse[:, 0:1]
 
     arrived(z_in.at[0:depth - 1], gz_recv, sibling)
     own_rows[...] = jnp.sum(z_in[...].astype(F32), axis=0) * inverse[0:1, 0:1]
@@ -510,6 +520,7 @@
     left(z_in.at[0:depth - 1], gz_send, sibling)
     left(extra_z.at[0:depth - 1], ez_send, sibling)
     left(extra_plane.at[0:planes - 1], ep_send, sibling)
+    extra_half.wait_send()
     extra_swap.wait_send()
     own_out.wait()
     arrived(part_proj.at[0:planes - 1], ga_recv, sibling)
@@ -562,16 +573,17 @@
         pltpu.VMEM((depth, 16, tile_cols), BF16),
         pltpu.VMEM((depth, 16, tile_cols), BF16),
         pltpu.VMEM((16, tile_cols), F32),
-        pltpu.VMEM((16, width), F32),
-        pltpu.VMEM((depth, 16, width), F32),
-        pltpu.VMEM((16, width), F32),
-        pltpu.VMEM((planes, 16, width), F32),
-        pltpu.VMEM((16, width), F32),
-        pltpu.VMEM((16, width), F32),
+        pltpu.VMEM((2, 8, width), F32),
+        pltpu.VMEM((8, width), F32),
+        pltpu.VMEM((8, width), F32),
+        pltpu.VMEM((depth, 8, width), F32),
+        pltpu.VMEM((8, width), F32),
+        pltpu.VMEM((planes, 8, width), F32),
+        pltpu.VMEM((2, 8, width), F32),
         one, one, one, dma(4), dma(2), one, one, one, one, one, one,
         one, dma(4), dma(2), one, dma(4), one, dma(4 * side), one, one,
-        one, dma(turns), one, one, one, one, one, one,
-        one, one, one, one, one, one, one, one, dma(6), dma(4),
+        one, dma(turns), one, one, one, dma(4), one, one,
+        one, one, one, one, one, one, one, one, one, one, dma(6), dma(4),
     ]
     grad, gout, loss = pl.pallas_call(
         functools.partial(step_kernel, (side, depth, blk, slots, hid)),

time: 77.5 us -> 76.1 us (0.982)
  Pallas kernels: 72.8 us -> 71.4 us
    pallas_call x1, Pallas kernels: 72.8 us -> 71.4 us  [shards(): pl.pallas_call(functools.partial(step_kernel, (side, depth, blk, slots, h...]
where the time goes in v7:
time: 76.1 us; the launch traced here: 76 us
  Pallas kernels  71.4 us (94%)
  between operations  2.41 us (3%)
  local copies, waits for them, and re-layouts  2.17 us (3%)
    pallas_call x1, Pallas kernels, shards(): pl.pallas_call(functools.partial(step_kernel, (side, depth, blk, slots, h...  71.4 us
    unnamed x4, local copies, waits for them, and re-layouts  2.17 us

profile of v7, /device:TPU:1, one launch (start us, length us, event | category | flops | bytes accessed | tf_op | source)
XLA Modules:
  0.0 76.0 jit_solution(9509624752339749184)
XLA Ops:
  0.6 71.4 %shard_map.112 = (f32[32,1024]{1,0:T(8,128)}, f32[8,128]{1,0:T(8,128)}, f32[1,1]{1,0:T(1,128)}) custom-call(bf16[1024,512]{1,0:T(8,128)(2,1)} %tiles_hbm.1, s32[1,1024]{1,0:T(1,128)} %bitcast.4, s32[16,64]{1,0:T(8,128)} %neighbors_hbm.1, s32[16]{0:T(128)} %counts_hbm.1, s32[16,64]{1,0:T(8,128)} %flows_hbm.1, bf16[16,1024]{1,0:T(8,128)(2,1)} %anchor_hbm.1, ...), custom_call_target="tpu_custom_call" | custom-call | flops 4294967296 | bytes 1048576 | tf_op jit(solution)/shard_map/pallas_call | solution.py:588
  72.1 0.0 copy-start
  72.1 1.6 %copy.15 = f32[32,1024]{1,0:T(8,128)} copy(f32[32,1024]{1,0:T(8,128)} %get-tuple-element.12) | data formatting | bytes 262144
  73.6 0.0 copy-done
  73.6 0.6 copy.16
Async XLA Ops:
  72.1 1.6 %copy-start = (f32[8,128]{1,0:T(8,128)S(1)}, f32[8,128]{1,0:T(8,128)}, u32[]{:S(2)}) copy-start(f32[8,128]{1,0:T(8,128)} %get-tuple-element.7) | copy-start | bytes 12292

commit v8 on v7

--- a/solution.py
+++ b/solution.py
@@ -31,7 +31,7 @@
     tiles_hbm, tile_block_hbm, neighbors_hbm, counts_hbm, flows_hbm, anchor_hbm, dest_hbm, hidden_hbm, out_hbm,
     grad_out, gout_out, loss_out,
     tiles, tile_block, neighbors, counts, flows, w_out,
-    weights, features, tile_w, plane_feats, part_proj, own_proj, window, proj, onehot, first, first_t, lanes, out_weight, active, pre, grad, sib_grad, chip_grad, u_in, u_sum, v_in,
+    weights, features, tile_w, plane_feats, part_proj, own_proj, window, proj, onehot, first, first_t, lanes, active, pre, grad, sib_grad, chip_grad, u_in, u_sum, v_in,
     plane_sum, z_in, own_rows, extra, extra_sib, extra_own, extra_z, extra_zsum, extra_plane, extra_all,
     halo_send, halo_recv, fz_send, fz_recv, fz_pass, fs_send, fs_recv, fp_send, fp_recv, pp_send, pp_recv,
     az_send, az_recv, az_pass, p1_send, p1_recv, p2_send, p2_recv, sb_send, sb_recv,
@@ -326,14 +326,12 @@
     each(0, turns, hidden)
     arrived(weights.at[:, 1 - core], sb_recv, sibling)
 
-    out_weight[...] = w_out[...].astype(F32).reshape(1, hid)
-
     def score(n):
         act = jnp.maximum(
             jnp.dot(first[...], weights[:, :, :, :, turn(n)].reshape(hid, wide), preferred_element_type=F32), 0.0
         )
         active[:, turn(n)] = act
-        part = act * out_weight[:, turn(n)]
+        part = act * w_out[:, turn(n)]
         lanes[...] += sum(part[:, k:k + 128] for k in range(0, wide, 128))
 
     lanes[...] = jnp.zeros_like(lanes)
@@ -342,7 +340,7 @@
     scores = jnp.zeros((slots, blk), F32)
     for b in range(blk):
         scores = jnp.where(lane16 == b, col[b * slots:(b + 1) * slots], scores)
-    weight = out_weight[...]
+    weight = w_out[...]
 
     top = jnp.max(jnp.where(valid, scores, -jnp.inf), axis=0, keepdims=True)
     expo = jnp.where(valid, jnp.exp(scores - top), 0.0)
@@ -548,7 +546,7 @@
         pltpu.VMEM((blk, slots), jnp.int32),
         pltpu.SMEM((blk,), jnp.int32),
         pltpu.VMEM((blk, slots), jnp.int32),
-        pltpu.VMEM((hid,), BF16),
+        pltpu.VMEM((1, hid), F32),
         pltpu.VMEM((depth, 2, 2, 16, hid), BF16),
         pltpu.VMEM((blk, feat), BF16),
         pltpu.VMEM((depth, 2, 16, tile_cols), BF16),
@@ -561,7 +559,6 @@
         pltpu.VMEM((pairs, hid), BF16),
         pltpu.VMEM((hid, pairs), BF16),
         pltpu.VMEM((pairs, 128), F32),
-        pltpu.VMEM((1, hid), F32),
         pltpu.VMEM((pairs, hid), F32),
         pltpu.VMEM((pairs, hid), BF16),
         pltpu.VMEM((depth, 2, 2, 16, hid), BF16),
@@ -601,7 +598,7 @@
         cost_estimate=pl.CostEstimate(
             flops=4 * pairs * hid * hid, bytes_accessed=2 * tiles.size, transcendentals=pairs
         ),
-    )(tiles, tile_block.reshape(1, -1), neighbors, counts, flows, w_anchor, w_dest, w_hidden, w_out)
+    )(tiles, tile_block.reshape(1, -1), neighbors, counts, flows, w_anchor, w_dest, w_hidden, w_out.astype(F32).reshape(1, -1))
     return grad, gout.reshape(hid), loss.reshape(())
 
 

time: 76.1 us -> 77.4 us (1.017)
  other arithmetic: 0 us -> 1.28 us
    reshape x0 -> x1, other arithmetic: none -> 1.28 us  [shards(): w_out.astype(F32).reshape(1, -1)]
where the time goes in v8:
time: 77.4 us; the launch traced here: 77.3 us
  Pallas kernels  71.4 us (92%)
  between operations  2.41 us (3%)
  local copies, waits for them, and re-layouts  2.17 us (3%)
  other arithmetic  1.28 us (2%)
    pallas_call x1, Pallas kernels, shards(): pl.pallas_call(functools.partial(step_kernel, (side, depth, blk, slots, h...  71.4 us
    unnamed x4, local copies, waits for them, and re-layouts  2.17 us

profile of v8, /device:TPU:1, one launch (start us, length us, event | category | flops | bytes accessed | tf_op | source)
XLA Modules:
  0.0 77.3 jit_solution(15024606492202102502)
XLA Ops:
  0.6 1.3 %reshape.25 = f32[1024]{0:T(1024)} convert(bf16[1024]{0:T(1024)(128)(2,1)} %param.17) | non-fusion elementwise | flops 1024 | bytes 6144 | tf_op jit(solution)/shard_map/reshape | solution.py:601
  1.9 71.4 %shard_map.112 = (f32[32,1024]{1,0:T(8,128)}, f32[8,128]{1,0:T(8,128)}, f32[1,1]{1,0:T(1,128)}) custom-call(bf16[1024,512]{1,0:T(8,128)(2,1)} %tiles_hbm.1, s32[1,1024]{1,0:T(1,128)} %bitcast.6, s32[16,64]{1,0:T(8,128)} %neighbors_hbm.1, s32[16]{0:T(128)} %counts_hbm.1, s32[16,64]{1,0:T(8,128)} %flows_hbm.1, bf16[16,1024]{1,0:T(8,128)(2,1)} %anchor_hbm.1, ...), custom_call_target="tpu_custom_call" | custom-call | flops 4294967296 | bytes 1048576 | tf_op jit(solution)/shard_map/pallas_call | solution.py:585
  73.3 0.0 copy-start
  73.3 1.6 %copy.15 = f32[32,1024]{1,0:T(8,128)} copy(f32[32,1024]{1,0:T(8,128)} %get-tuple-element.12) | data formatting | bytes 262144
  74.9 0.0 copy-done
  74.9 0.6 copy.16
Async XLA Ops:
  73.3 1.6 %copy-start = (f32[8,128]{1,0:T(8,128)S(1)}, f32[8,128]{1,0:T(8,128)}, u32[]{:S(2)}) copy-start(f32[8,128]{1,0:T(8,128)} %get-tuple-element.7) | copy-start | bytes 12292
